TPU v7x, 32 devices: a whole 2x2x4 slice. The times are simulated.
32 devices in a mesh: span: 8 (over z, x), elem: 4 (over y, core).
Axes of the slice: x: 2, y: 2, z: 4, core: 2. Of those that a mesh axis runs over, the one named last changes fastest.
Arguments:
- species: float32 [81, 3, 512, 512], P(None, None, 'span', 'elem'), may hold values from 0.02 to 0.3
- laplacian: float32 [81, 3, 512, 512], P(None, None, 'span', 'elem'), may hold values from -6 to 6
- binary: float32 [3, 4], replicated, may hold values from 0.3 to 3
- dref: float32 [3], replicated, may hold values from 0.5 to 2
- stiff_eig: float32 [9], replicated, may hold values from 0.02 to 3
- basis: float32 [9, 9], replicated, may hold values from -1 to 1, as said below
- rounds: int32 [256], replicated, may hold values from 1 to 4
- adjacency: int32 [512, 4], P('elem'), may hold values from 0 to 511, as said below
- edge_map: int32 [512, 4], P('elem'), may hold values from 0 to 3
Outputs:
- updated: float32 [81, 3, 512, 512], P(None, None, 'span', 'elem')
Inputs may be any that keep to these rules, and one draw needn't show every extreme that they name: basis is an orthogonal matrix. The elements form a periodic mesh of 16 columns and 8 * 4 rows; each index of elem holds 8 whole rows in some order. adjacency is symmetric: element e lies across edge edge_map[e, j] of element adjacency[e, j]. The element across an edge lies on the same index of elem or on the one just before or after it, cyclically; exactly 16 elements of each index have an edge facing the next index and 16 one facing the previous, one such edge each.
All inputs are finite; a program needn't handle non-finite values.
Results may differ from a plain program's by a relative error of at most 0.0001.
Values sent between devices are 32-bit elements; how exact they have to be, the bound alone decides.
No kernel may reach another device: no remote copies, remote signals or barrier semaphores. Data moves between devices by JAX's collectives and lax.ppermute only.
A program may use at most 128 MiB of HBM per device.

v0:
```python
import functools

import jax
import jax.numpy as jnp
import numpy as np
from jax import lax
from jax.experimental import pallas as pl
from jax.experimental.pallas import tpu as pltpu
from jax.sharding import PartitionSpec as P

MESH_X = 16
LANES = 128
SIDE = 9
PAIRS = 8
QUAD = 4
NODE_ROWS = 88
TRACE_ROWS = 40
N_SWEEPS = 3
WHOLE = 2
COST_SCALE = 5
FIRST_WHOLE = True
DONE = jax.ShapeDtypeStruct((8, LANES), jnp.float32)
VMEM_BYTES = 60 * 1024 * 1024
UNPACK_BYTES = 48 * 1024 * 1024


coupling = 0.2
highest = lax.Precision.HIGHEST
two_pi = 6.283185307179586
f32 = jnp.float32
bf16 = jnp.bfloat16


def edge_lists(per_side):
    last_node = per_side - 1
    bottom = [i for i in range(per_side)]
    right_edge = [i * per_side + last_node for i in range(per_side)]
    top_edge = [last_node * per_side + last_node - i for i in range(per_side)]
    left_edge = [(last_node - i) * per_side for i in range(per_side)]
    return [bottom, right_edge, top_edge, left_edge]


def row_orders(n_span):
    even = [r ^ (r >> 1 & 1) for r in range(n_span)]
    odd = [r ^ int(2 * r >= n_span) for r in range(n_span)][::-1]
    return [even, odd]


def ring_route(n_span, n_elem, step):
    orders = row_orders(n_span)
    places = [orders[p % 2][r] * n_elem + p for p in range(n_elem) for r in range(n_span)]
    count = len(places)
    return [(places[g], places[(g + step) % count]) for g in range(count)]


def lasting(micros):
    return pl.CostEstimate(flops=int(micros * COST_SCALE * 1150000000), bytes_accessed=0, transcendentals=0)


def split_terms(values):
    top = values.astype(bf16)
    return top, (values - top.astype(f32)).astype(bf16)


def half_swap(first, second):
    low = lax.broadcasted_iota(jnp.int32, first.shape, 1) < LANES // 2
    left = jnp.where(low, first, pltpu.roll(second, LANES // 2, 1))
    right = jnp.where(low, pltpu.roll(first, LANES // 2, 1), second)
    return left, right


def tables_kernel(
    n_span, n_elem, adj_ref, map_ref, perm_ref, perm2_ref, base_ref, step_ref, send_ref
):
    own = adj_ref.shape[1]
    span_id, elem_id = lax.axis_index("span"), lax.axis_index("elem")
    lane = lax.broadcasted_iota(jnp.int32, (own, own), 1).astype(f32)
    sub = lax.broadcasted_iota(jnp.int32, (own, own), 0).astype(f32)
    eye = (lane == sub).astype(f32)
    first_own = (elem_id * own).astype(f32)
    first_next = (lax.rem(elem_id + 1, n_elem) * own).astype(f32)
    first_prev = (lax.rem(elem_id + n_elem - 1, n_elem) * own).astype(f32)

    def column(row):
        return jnp.sum(eye * row, axis=1, keepdims=True)

    def inside(ids, first):
        return (ids >= first) & (ids < first + own)

    adj_row = [adj_ref[j : j + 1, :].astype(f32) for j in range(4)]
    map_row = [map_ref[j : j + 1, :].astype(f32) for j in range(4)]
    meets = [(sub == adj_row[j] - first_own).astype(f32) for j in range(4)]
    near = (eye + meets[0] + meets[1] + meets[2] + meets[3]).astype(bf16)
    prev_row = jnp.zeros((1, own), f32)
    next_row = jnp.zeros((1, own), f32)
    for j in range(4):
        prev_row = prev_row + jnp.where(inside(adj_row[j], first_prev), adj_row[j] + 1.0, 0.0)
        next_row = next_row + jnp.where(inside(adj_row[j], first_next), adj_row[j] + 1.0, 0.0)
    prev_col, next_col = column(prev_row), column(next_row)
    reached = jnp.broadcast_to((prev_col > 0).astype(f32), (own, own))
    row_col = 1.0 - reached
    for _ in range(n_span - 2):
        reached = jnp.minimum(
            jnp.dot(near, reached.astype(bf16), preferred_element_type=f32), 1.0
        )
        row_col = row_col + 1.0 - reached
    row_row = jnp.sum(eye * row_col, axis=0, keepdims=True)
    same = row_col == row_row
    pos_col = jnp.sum((same & (lane < sub)).astype(f32), axis=1, keepdims=True)
    pos_row = jnp.sum((same & (sub < lane)).astype(f32), axis=0, keepdims=True)
    odd = lax.rem(elem_id, 2) == 1
    orders = row_orders(n_span)
    slot_row = jnp.zeros_like(row_row)
    for r in range(n_span):
        slot = jnp.where(odd, orders[1][r], orders[0][r]).astype(f32)
        slot_row = jnp.where(row_row == float(r), slot, slot_row)
    new_row = slot_row * float(MESH_X) + pos_row
    perm = (sub == new_row).astype(f32).astype(bf16)
    perm_ref[:, :own] = perm
    perm_ref[:, own:] = perm
    perm2_ref[:own] = perm
    perm2_ref[own:] = perm

    def rank(col, row):
        return jnp.sum(((col > 0) & (col < row)).astype(f32), axis=0, keepdims=True)

    rank_prev, rank_next = rank(prev_col, prev_row), rank(next_col, next_row)
    spot = lax.broadcasted_iota(jnp.int32, (MESH_X, own), 0).astype(f32)
    here = new_row == spot + (span_id * MESH_X).astype(f32)
    edge_up = jnp.zeros_like(row_row)
    edge_down = jnp.zeros_like(row_row)

    def chosen(values):
        picks = jnp.sum(jnp.where(here, values, 0.0), axis=1, keepdims=True)
        return jnp.broadcast_to(picks, (MESH_X, own))

    per_elem = float(TRACE_ROWS)
    per_row = MESH_X * per_elem
    side_rows = float(MESH_X * SIDE)
    for j in range(4):
        its_pos = jnp.sum(meets[j] * pos_col, axis=0, keepdims=True)
        its_row = jnp.sum(meets[j] * row_col, axis=0, keepdims=True)
        inner = inside(adj_row[j], first_own)
        ahead = inside(adj_row[j], first_next)
        behind = inside(adj_row[j], first_prev)
        up = ahead | (inner & (its_row == row_row + 1.0))
        down = behind | (inner & (its_row == row_row - 1.0))
        its_pos = jnp.where(ahead, rank_next, jnp.where(behind, rank_prev, its_pos))
        base = jnp.where(
            up,
            per_row + its_pos,
            jnp.where(down, per_row + side_rows + its_pos, its_pos * per_elem + map_row[j]),
        )
        edge_up = jnp.where(up, float(j), edge_up)
        edge_down = jnp.where(down, float(j), edge_down)
        rows = slice(j * MESH_X, (j + 1) * MESH_X)
        base_ref[rows] = chosen(base)
        step_ref[rows] = chosen(jnp.where(up | down, float(MESH_X), 4.0))
    send_ref[:MESH_X] = chosen(edge_up) + spot * per_elem
    send_ref[MESH_X:] = chosen(edge_down) + spot * per_elem


def mesh_tables(adjacency, edge_map, n_span, n_elem):
    own = adjacency.shape[0]
    return pl.pallas_call(
        functools.partial(tables_kernel, n_span, n_elem),
        out_shape=(
            jax.ShapeDtypeStruct((own, 2 * own), bf16),
            jax.ShapeDtypeStruct((2 * own, own), bf16),
            jax.ShapeDtypeStruct((4 * MESH_X, own), f32),
            jax.ShapeDtypeStruct((4 * MESH_X, own), f32),
            jax.ShapeDtypeStruct((2 * MESH_X, own), f32),
        ),
        in_specs=[
            pl.BlockSpec(memory_space=pltpu.VMEM),
            pl.BlockSpec(memory_space=pltpu.VMEM),
        ],
        out_specs=[pl.BlockSpec(memory_space=pltpu.VMEM)] * 5,
        cost_estimate=lasting(3),
        name="mesh_tables",
    )(adjacency.T, edge_map.T)


def link_kernel(
    base_ref, step_ref, send_ref, from_ref, turn_ref, skip_ref, out_ref, move_ref, link_ref, pick_ref
):
    def spread(table, values):
        return jnp.dot(table[...], values[...], precision=highest, preferred_element_type=f32)

    def fill(ref, wanted):
        for c in range(0, ref.shape[1], LANES):
            width = min(LANES, ref.shape[1] - c)
            lane = lax.broadcasted_iota(jnp.int32, wanted.shape, 1).astype(f32) + float(c)
            ref[:, c : c + width] = (wanted == lane).astype(f32).astype(bf16)[:, :width]

    fill(link_ref, spread(from_ref, base_ref) + turn_ref[...] * spread(from_ref, step_ref) + skip_ref[...])
    fill(pick_ref, spread(out_ref, send_ref) + move_ref[...])


def link_matrices(base, step, send, own):
    rows = MESH_X * TRACE_ROWS
    from_edge = np.zeros((rows, 4 * MESH_X), np.float32)
    turn = np.zeros((rows, own), np.float32)
    skip = np.full((rows, own), -1.0, np.float32)
    for i in range(MESH_X):
        for t in range(SIDE):
            for j in range(4):
                row = i * TRACE_ROWS + t * 4 + j
                from_edge[row, j * MESH_X + i] = 1.0
                turn[row] = SIDE - 1 - t
                skip[row] = 0.0
    side_rows = SIDE * MESH_X
    out_edge = np.zeros((2 * side_rows, 2 * MESH_X), np.float32)
    move = np.zeros((2 * side_rows, own), np.float32)
    for way in range(2):
        for t in range(SIDE):
            for i in range(MESH_X):
                row = way * side_rows + t * MESH_X + i
                out_edge[row, way * MESH_X + i] = 1.0
                move[row] = 4 * t
    vmem = pl.BlockSpec(memory_space=pltpu.VMEM)
    return pl.pallas_call(
        link_kernel,
        out_shape=(
            jax.ShapeDtypeStruct((rows, rows + 2 * side_rows), bf16),
            jax.ShapeDtypeStruct((2 * side_rows, rows), bf16),
        ),
        in_specs=[vmem] * 8,
        out_specs=[vmem] * 2,
        cost_estimate=lasting(4),
        name="link_matrices",
    )(base, step, send, from_edge, turn, skip, out_edge, move)


def source_kernel(s, part, binary_ref, dref_ref, species_ref, lap_ref, perm_ref, *refs):
    out_ref, done_ref = refs[-2:]
    done_ref[...] = jnp.zeros_like(done_ref)
    per_step, n_species, zl, own = species_ref.shape
    n_span = out_ref.shape[0]
    perm = perm_ref[...]

    def inverse(value):
        return 1.0 / jnp.full((8, own), value, f32)

    def wide(row):
        return jnp.broadcast_to(row[:1], (zl, own))

    scaled = [dref_ref[s] * inverse(binary_ref[s, j]) for j in range(n_species + 1)]
    bath = wide(scaled[n_species])
    other = [wide(scaled[j] - scaled[n_species]) for j in range(n_species)]
    inv_dref = wide(inverse(dref_ref[s]))

    def source(n):
        parts = [species_ref[n, j] for j in range(n_species)]
        resistance = bath - bath * parts[s]
        for j in range(n_species):
            if j != s:
                resistance = resistance + parts[j] * other[j]
        mixture = (1.0 - parts[s]) * pl.reciprocal(resistance, approx=False)
        return parts[s] * inv_dref + (mixture - 1.0) * lap_ref[n, 0]

    def turned(first, second):
        top, rest = split_terms(jnp.concatenate([first, second], axis=0))
        both = jnp.concatenate([top, rest], axis=1)
        return lax.dot_general(
            perm, both, (((1,), (1,)), ((), ())), preferred_element_type=f32
        )

    def blocks():
        pairs = per_step // 2
        for k in range(pairs):
            tile = turned(source(2 * k), source(2 * k + 1))
            for q in range(n_span):
                rows = block_rows(part, k, pairs)
                out_ref[q, rows, :] = tile[q * MESH_X : (q + 1) * MESH_X]

    def tail():
        value = source(0)
        tile = turned(value, value)
        half = MESH_X // 2
        low = lax.broadcasted_iota(jnp.int32, (half, 2 * zl), 1) < zl
        for q in range(n_span):
            block = tile[q * MESH_X : (q + 1) * MESH_X]
            out_ref[q, :half, :] = jnp.where(low, block[:half], block[half:])

    by_step(part > 0, blocks, tail)


def block_rows(part, k, pairs):
    if part == WHOLE:
        return slice(k * MESH_X, (k + 1) * MESH_X)
    return pl.ds(k, MESH_X, stride=pairs)


def by_step(has_tail, blocks, tail):
    if not has_tail:
        blocks()
        return
    last_step = pl.num_programs(0) - 1
    pl.when(pl.program_id(0) < last_step)(blocks)
    pl.when(pl.program_id(0) == last_step)(tail)


def part_blocks(n_nodes, part):
    groups = n_nodes // (2 * PAIRS)
    rows = MESH_X * PAIRS
    first = groups // 2
    if part == 0:
        return 0, first, first * rows
    if part == WHOLE:
        return 0, groups + 1, groups * rows + MESH_X // 2
    return first, groups - first + 1, (groups - first) * rows + MESH_X // 2


def packed_source(s, part, species, laplacian, binary, dref, perm, n_span, after):
    n_nodes, n_species, zl, own = species.shape
    step = 2 * PAIRS
    begin, steps, rows = part_blocks(n_nodes, part)
    return pl.pallas_call(
        functools.partial(source_kernel, s, part),
        grid=(steps,),
        out_shape=(jax.ShapeDtypeStruct((n_span, rows, 2 * zl), f32), DONE),
        in_specs=[
            pl.BlockSpec(memory_space=pltpu.SMEM),
            pl.BlockSpec(memory_space=pltpu.SMEM),
            pl.BlockSpec((step, n_species, zl, own), lambda g: (g + begin, 0, 0, 0)),
            pl.BlockSpec((step, 1, zl, own), lambda g: (g + begin, s, 0, 0)),
            pl.BlockSpec((own, 2 * own), lambda g: (0, 0)),
        ]
        + [pl.BlockSpec(memory_space=pl.ANY)] * len(after),
        out_specs=(
            pl.BlockSpec((n_span, MESH_X * PAIRS, 2 * zl), lambda g: (0, g, 0)),
            pl.BlockSpec(DONE.shape, lambda g: (0, 0)),
        ),
        compiler_params=pltpu.CompilerParams(vmem_limit_bytes=VMEM_BYTES),
        cost_estimate=lasting(4),
        name="packed_source",
    )(binary, dref, species, laplacian, perm, *after)


def unpack_kernel(part, recv_ref, perm_ref, *refs):
    out_ref = refs[-1]
    n_span = recv_ref.shape[0]
    per_step, _, zl, _ = out_ref.shape
    perm = perm_ref[...]

    def turned(tile):
        top, rest = split_terms(tile)
        both = jnp.concatenate([top, rest], axis=0)
        return lax.dot_general(
            both, perm, (((0,), (0,)), ((), ())), preferred_element_type=f32
        )

    def blocks():
        pairs = per_step // 2
        for k in range(pairs):
            tile = jnp.concatenate(
                [recv_ref[q, block_rows(part, k, pairs), :] for q in range(n_span)], axis=0
            )
            result = turned(tile)
            out_ref[2 * k, 0] = result[:zl]
            out_ref[2 * k + 1, 0] = result[zl:]

    def tail():
        half = MESH_X // 2
        sides = []
        for q in range(n_span):
            block = recv_ref[q, :half, :]
            sides += [block, pltpu.roll(block, zl, 1)]
        out_ref[0, 0] = turned(jnp.concatenate(sides, axis=0))[:zl]

    by_step(part > 0, blocks, tail)


def unpacked(s, part, recv, perm2, shape, before):
    n_nodes, n_species, zl, own = shape
    n_span, _, width = recv.shape
    step = 2 * PAIRS
    begin, steps, _ = part_blocks(n_nodes, part)
    operands = [recv, perm2] + ([] if before is None else [before])
    return pl.pallas_call(
        functools.partial(unpack_kernel, part),
        grid=(steps,),
        out_shape=jax.ShapeDtypeStruct(shape, f32),
        in_specs=[
            pl.BlockSpec((n_span, MESH_X * PAIRS, width), lambda g: (0, g, 0)),
            pl.BlockSpec((2 * own, own), lambda g: (0, 0)),
        ]
        + ([] if before is None else [pl.BlockSpec(memory_space=pl.ANY)]),
        out_specs=pl.BlockSpec((step, 1, zl, own), lambda g: (g + begin, s, 0, 0)),
        input_output_aliases={} if before is None else {2: 0},
        compiler_params=pltpu.CompilerParams(vmem_limit_bytes=UNPACK_BYTES),
        cost_estimate=lasting(0.1),
        name="unpacked",
    )(*operands)


def left_product(matrix, values):
    rows = matrix.shape[0] // 2
    top, rest = split_terms(values)
    both = jnp.dot(matrix, top, preferred_element_type=f32)
    return both[:rows] + both[rows:] + jnp.dot(matrix[:rows], rest, preferred_element_type=f32)


def right_product(values, top_ref, rest_ref):
    rows = values.shape[0]
    top, rest = split_terms(values)
    both = jnp.dot(jnp.concatenate([top, rest], axis=0), top_ref[...], preferred_element_type=f32)
    return both[:rows] + both[rows:] + jnp.dot(top, rest_ref[...], preferred_element_type=f32)


def chunk_rows(index, size):
    return pl.ds(pl.multiple_of(index * size, size), size)


def send_traces(trace_ref, pick_ref, up_ref, down_ref):
    top, rest = split_terms(trace_ref[...])
    out = jnp.dot(pick_ref[...], top, preferred_element_type=f32)
    out = out + jnp.dot(pick_ref[...], rest, preferred_element_type=f32)
    half = up_ref.shape[0]
    up_ref[...] = out[:half]
    down_ref[...] = out[half:]


def sent_block(sent, g, i):
    if len(sent) == 1:
        return sent[0], pl.ds(g * MESH_X * PAIRS + i, PAIRS, stride=MESH_X)
    before = sent[0].shape[1] // (MESH_X * PAIRS)
    if g < before:
        return sent[0], chunk_rows(g * MESH_X + i, PAIRS)
    return sent[1], chunk_rows((g - before) * MESH_X + i, PAIRS)


def sent_tail(sent):
    half = MESH_X // 2
    groups = sum(ref.shape[1] - half * (ref is sent[-1]) for ref in sent) // (MESH_X * PAIRS)
    return groups, sent[-1], sent[-1].shape[1] - half


def start_kernel(*refs):
    *sent, top_ref, rest_ref, diag_ref, eigen_ref, edge_ref, pick_ref = refs[:-6]
    w_ref, trace_ref, up_ref, down_ref, x, ends = refs[-6:]
    n_span = sent[0].shape[0]
    half = MESH_X // 2
    groups, late_ref, tail = sent_tail(sent)
    first = lax.broadcasted_iota(jnp.int32, (8, x.shape[1]), 0) == 0
    for tile in range(n_span // 2):
        lanes = slice(tile * LANES, (tile + 1) * LANES)
        left, right = half_swap(late_ref[2 * tile, tail:, :], late_ref[2 * tile + 1, tail:, :])
        ends[:half, lanes] = left
        ends[half:, lanes] = right

    def quad(c, carry):
        for ii in range(QUAD):
            i = c * QUAD + ii
            for tile in range(n_span // 2):
                lanes = slice(tile * LANES, (tile + 1) * LANES)
                for g in range(groups):
                    ref, block = sent_block(sent, g, i)
                    left, right = half_swap(ref[2 * tile, block, :], ref[2 * tile + 1, block, :])
                    base = ii * NODE_ROWS + g * PAIRS
                    x[base : base + PAIRS, lanes] = left
                    base += groups * PAIRS
                    x[base : base + PAIRS, lanes] = right
            base = ii * NODE_ROWS + 2 * groups * PAIRS
            x[base : base + 8, :] = jnp.where(first, ends[pl.ds(i, 1), :], 0.0)
        y = right_product(x[...], top_ref, rest_ref)
        for p in range(QUAD // 2):
            part = slice(p * 2 * NODE_ROWS, (p + 1) * 2 * NODE_ROWS)
            w = left_product(eigen_ref[...], y[part])
            pair = c * (QUAD // 2) + p
            w_ref[chunk_rows(pair, 2 * NODE_ROWS), :] = w
            trace_ref[chunk_rows(pair, 2 * TRACE_ROWS), :] = left_product(
                edge_ref[...], w * diag_ref[...]
            )
        return carry

    lax.fori_loop(0, MESH_X // QUAD, quad, 0, unroll=True)
    send_traces(trace_ref, pick_ref, up_ref, down_ref)


def fill_sources(trace_ref, above_ref, below_ref, top, rest):
    row = 0
    for ref in (trace_ref, above_ref, below_ref):
        block = slice(row, row + ref.shape[0])
        top[block], rest[block] = split_terms(ref[...])
        row += ref.shape[0]


def met_traces(link_ref, top, rest, met):
    met[...] = jnp.dot(link_ref[...], top[...], preferred_element_type=f32) + jnp.dot(
        link_ref[...], rest[...], preferred_element_type=f32
    )


def sweep_kernel(sweep_id, rounds_ref, diag_ref, link_ref, pick_ref, inner_ref, edge_ref, *refs):
    begun = sweep_id > 1
    start_ref, trace_ref, above_ref, below_ref = refs[:4]
    held_ref = refs[4] if begun else None
    kept_ref, tout_ref, up_ref, down_ref, top, rest, gathered = refs[5 if begun else 4 :]
    fill_sources(trace_ref, above_ref, below_ref, top, rest)
    met_traces(link_ref, top, rest, gathered)
    going = rounds_ref[...] > sweep_id

    def quad(c, carry):
        rows = chunk_rows(c, QUAD * TRACE_ROWS)
        met = gathered[rows, :]
        kept_ref[rows, :] = jnp.where(going, met, held_ref[rows, :] if begun else 0.0)
        for p in range(QUAD // 2):
            part = met[p * 2 * TRACE_ROWS : (p + 1) * 2 * TRACE_ROWS]
            field = left_product(inner_ref[...], part) * diag_ref[...]
            rows = chunk_rows(c * (QUAD // 2) + p, 2 * TRACE_ROWS)
            tout_ref[rows, :] = start_ref[rows, :] + left_product(edge_ref[...], field)
        return carry

    lax.fori_loop(0, MESH_X // QUAD, quad, 0, unroll=True)
    send_traces(tout_ref, pick_ref, up_ref, down_ref)


def finish_kernel(
    sweep_id, rounds_ref, diag_ref, link_ref, inner_ref, nodal_ref, trace_ref, above_ref,
    below_ref, held_ref, w_ref, top_ref, rest_ref, *refs,
):
    *sent, top, rest, gathered, modal, ends = refs
    n_span = sent[0].shape[0]
    half = MESH_X // 2
    groups, late_ref, tail = sent_tail(sent)
    fill_sources(trace_ref, above_ref, below_ref, top, rest)
    met_traces(link_ref, top, rest, gathered)
    going = rounds_ref[...] > sweep_id

    def quad(c, carry):
        rows = chunk_rows(c, QUAD * TRACE_ROWS)
        kept = jnp.where(going, gathered[rows, :], held_ref[rows, :])
        for p in range(QUAD // 2):
            part = kept[p * 2 * TRACE_ROWS : (p + 1) * 2 * TRACE_ROWS]
            rows = chunk_rows(c * (QUAD // 2) + p, 2 * NODE_ROWS)
            field = (w_ref[rows, :] + left_product(inner_ref[...], part)) * diag_ref[...]
            modal[p * 2 * NODE_ROWS : (p + 1) * 2 * NODE_ROWS] = left_product(
                nodal_ref[...], field
            )
        z = right_product(modal[...], top_ref, rest_ref)
        for ii in range(QUAD):
            i = c * QUAD + ii
            for tile in range(n_span // 2):
                lanes = slice(tile * LANES, (tile + 1) * LANES)
                for g in range(groups):
                    base = ii * NODE_ROWS + g * PAIRS
                    later = base + groups * PAIRS
                    left, right = half_swap(
                        z[base : base + PAIRS, lanes], z[later : later + PAIRS, lanes]
                    )
                    ref, block = sent_block(sent, g, i)
                    ref[2 * tile, block, :] = left
                    ref[2 * tile + 1, block, :] = right
            base = ii * NODE_ROWS + 2 * groups * PAIRS
            ends[pl.ds(i, 1), :] = z[base : base + 1]
        return carry

    lax.fori_loop(0, MESH_X // QUAD, quad, 0, unroll=True)
    for tile in range(n_span // 2):
        lanes = slice(tile * LANES, (tile + 1) * LANES)
        left, right = half_swap(ends[:half, lanes], ends[half:, lanes])
        late_ref[2 * tile, tail:, :] = left
        late_ref[2 * tile + 1, tail:, :] = right


def vmem_call(kernel, name, out_shape, scratch, micros, operands, after):
    count, extra = len(operands), len(after)

    def ordered(*refs):
        last = count + extra + len(out_shape)
        refs[last][...] = jnp.zeros_like(refs[last])
        kernel(*refs[:count], *refs[count + extra : last], *refs[last + 1 :])

    vmem = pl.BlockSpec(memory_space=pltpu.VMEM)
    return pl.pallas_call(
        ordered,
        out_shape=tuple(out_shape) + (DONE,),
        in_specs=[vmem] * count + [pl.BlockSpec(memory_space=pl.ANY)] * extra,
        out_specs=tuple([vmem] * (len(out_shape) + 1)),
        scratch_shapes=scratch,
        compiler_params=pltpu.CompilerParams(vmem_limit_bytes=VMEM_BYTES),
        cost_estimate=lasting(micros),
        name=name,
    )(*operands, *after)


def stacked_terms(values):
    return jnp.concatenate(outer_split(values), axis=0)


def twice(matrix):
    zero = jnp.zeros_like(matrix)
    return jnp.concatenate(
        [jnp.concatenate([matrix, zero], axis=1), jnp.concatenate([zero, matrix], axis=1)], axis=0
    )


def nodal_matrices(basis):
    m = basis.shape[0]
    n_nodes = m * m
    kron_basis = (basis[:, None, :, None] * basis[None, :, None, :]).reshape(n_nodes, n_nodes)
    order = np.concatenate(
        [np.arange(0, n_nodes - 1, 2), np.arange(1, n_nodes - 1, 2), [n_nodes - 1]]
    )
    edges = np.array(edge_lists(m)).T.reshape(-1)
    full, edge = NODE_ROWS - n_nodes, TRACE_ROWS - edges.size
    nodal = jnp.pad(kron_basis[order], ((0, full), (0, full)))
    traces = jnp.pad(kron_basis[edges], ((0, edge), (0, full)))
    return [
        stacked_terms(twice(matrix)) for matrix in (nodal.T, traces, coupling * traces.T, nodal)
    ]


def solve_stages(n_sweeps, arrived, sent_shapes, rounds_row, diag, link, pick, matrices, forward, backward):
    eigen, edge, inner, nodal = matrices
    planes = forward[0].shape[0]
    w_shape = jax.ShapeDtypeStruct((MESH_X * NODE_ROWS, planes), f32)
    trace = jax.ShapeDtypeStruct((MESH_X * TRACE_ROWS, planes), f32)
    side = jax.ShapeDtypeStruct((MESH_X * SIDE, planes), f32)
    sources = pltpu.VMEM((link.shape[1], planes), bf16)
    gathered = pltpu.VMEM(trace.shape, f32)
    quad = pltpu.VMEM((QUAD * NODE_ROWS, planes), f32)
    ends = pltpu.VMEM((MESH_X, planes), f32)
    axes = ("span", "elem")
    n_span, n_elem = lax.axis_size("span"), lax.axis_size("elem")

    def exchange(up, down):
        below = lax.ppermute(up, axes, ring_route(n_span, n_elem, 1))
        above = lax.ppermute(down, axes, ring_route(n_span, n_elem, -1))
        return above, below

    after = yield None
    w, start, up, down, mark = vmem_call(
        start_kernel,
        "start_solve",
        [w_shape, trace, side, side],
        [quad, ends],
        16,
        arrived + [forward[0], forward[1], diag, eigen, edge, pick],
        after,
    )
    traces, held = start, []
    for sweep_id in range(1, n_sweeps):
        above, below = exchange(up, down)
        after = yield mark, None
        kept, traces, up, down, mark = vmem_call(
            functools.partial(sweep_kernel, sweep_id),
            "sweep_solve",
            [trace, trace, side, side],
            [sources, sources, gathered],
            10,
            [rounds_row, diag, link, pick, inner, edge, start, traces, above, below] + held,
            after,
        )
        held = [kept]
    above, below = exchange(up, down)
    after = yield mark, None
    *result, mark = vmem_call(
        functools.partial(finish_kernel, n_sweeps),
        "finish_solve",
        [jax.ShapeDtypeStruct(shape, f32) for shape in sent_shapes],
        [sources, sources, gathered, quad, ends],
        17,
        [rounds_row, diag, link, inner, nodal, traces, above, below, kept, w]
        + [backward[0], backward[1]],
        after,
    )
    yield mark, result


def transform_terms(planes):
    modes = np.tile(np.arange(planes // 2), 2)
    angles = np.arange(planes)[:, None] * modes[None, :] % planes * (2 * np.pi / planes)
    real = np.arange(planes)[None, :] < planes // 2
    table = np.where(real, np.cos(angles), -np.sin(angles))
    weights = np.where(modes == 0, 1.0, 2.0)

    def terms(values):
        top = values.astype(bf16)
        return top, (values - top.astype(np.float64)).astype(bf16)

    return terms(table / planes), terms((table * weights[None, :]).T)


def outer_split(values):
    top = lax.reduce_precision(values, exponent_bits=8, mantissa_bits=7)
    return top.astype(bf16), (values - top).astype(bf16)


def row_body(species, laplacian, binary, dref, stiff_eig, basis, rounds, adjacency, edge_map):
    n_nodes, n_species, zl, own = species.shape
    n_span = lax.axis_size("span")
    n_elem = lax.axis_size("elem")
    planes = zl * n_span
    n_modes = planes // 2
    perm, perm2, base, step, send = mesh_tables(adjacency, edge_map, n_span, n_elem)

    def across(sent):
        return lax.all_to_all(sent, "span", split_axis=0, concat_axis=0, tiled=True)

    link, pick = link_matrices(base, step, send, own)
    matrices = nodal_matrices(basis)
    forward, backward = transform_terms(planes)
    col_mode = jnp.tile(jnp.arange(n_modes, dtype=jnp.int32), 2)
    wavenumber = col_mode.astype(f32) * (8.0 / planes)
    shifts = 1.0 / dref[:, None] + (wavenumber * wavenumber)[None, :]
    eig_sum = (stiff_eig[:, None] + stiff_eig[None, :]).reshape(n_nodes)
    eig_sum = jnp.tile(jnp.pad(eig_sum, (0, NODE_ROWS - n_nodes)), 2)
    diag = 1.0 / (shifts[:, None, :] + eig_sum[None, :, None])
    rounds_row = jnp.tile(rounds, 2).reshape(1, planes)

    in_parts = [(WHOLE,) if FIRST_WHOLE and s == 0 else (0, 1) for s in range(n_species)]
    out_parts = [(WHOLE,) if s + 1 == n_species else (0, 1) for s in range(n_species)]
    steps, count = [], 0
    arrived_by, slots, back_slots = [], [], []
    for parts, slot_list in ((in_parts, slots), (out_parts, back_slots)):
        for group in parts:
            slot_list.append(range(count, count + len(group)))
            count += len(group)
    in_count = slots[-1][-1] + 1
    for s in range(n_species):
        for slot, part in zip(slots[s], in_parts[s]):
            early = min(slot - 2, slots[0][-1] - 1) if slot < 3 else slots[0][-1] - 1
            steps.append((early if slot else -2, 2, slot, s, ("pack", part)))
        first = slots[s][-1]
        for stage in range(N_SWEEPS + 1):
            steps.append((first + stage, 0, s, s, ("solve", stage)))
        for slot, part in zip(back_slots[s], out_parts[s]):
            steps.append((slot, 1, slot, s, ("unpack", part)))
    moved, waiting, solves, mark = [], [], [], []
    updated, last = None, -2
    for arrival, _, _, s, (kind, index) in sorted(steps):
        if arrival > last and waiting:
            final = len(moved) + 1 == count
            moved.append(across(released(waiting.pop(0), mark + (moved[-1:] if final else []))))
        last = arrival
        after = mark + (moved[arrival : arrival + 1] if arrival >= 0 else [])
        if kind == "pack":
            sent, done = packed_source(
                s, index, species, laplacian, binary, dref, perm, n_span, after
            )
            waiting.append(sent)
            mark = [done]
        elif kind == "solve":
            if index == 0:
                shapes = [
                    (n_span, part_blocks(n_nodes, part)[2], 2 * zl) for part in out_parts[s]
                ]
                solves.append(
                    solve_stages(
                        N_SWEEPS, [moved[slot] for slot in slots[s]], shapes, rounds_row, diag[s],
                        link, pick, matrices, forward, backward,
                    )
                )
                next(solves[s])
            done, result = solves[s].send(after)
            mark = [done]
            if result is not None:
                waiting += result
        else:
            updated = unpacked(s, index, moved[arrival], perm2, species.shape, updated)
    return updated


def released(block, after):
    def kernel(*refs):
        pass

    anywhere = pl.BlockSpec(memory_space=pl.ANY)
    return pl.pallas_call(
        kernel,
        out_shape=jax.ShapeDtypeStruct(block.shape, block.dtype),
        in_specs=[anywhere] * (1 + len(after)),
        out_specs=anywhere,
        input_output_aliases={0: 0},
        name="released",
    )(block, *after)


def from_behind(block, axis, distance):
    devices = range(lax.axis_size(axis))
    route = [((i - distance) % len(devices), i) for i in devices]
    return lax.ppermute(block, axis, route)


def edge_matrix(per_side):
    edge_table = np.zeros((4, per_side, per_side * per_side), np.float32)
    for edge_id, node_list in enumerate(edge_lists(per_side)):
        for i, node_id in enumerate(node_list):
            edge_table[edge_id, i, node_id] = 1.0
    return edge_table


def mixture_source(species, laplacian, binary, dref):
    n_species = species.shape[1]
    bath_share = 1.0 - jnp.sum(species, axis=1)
    source_parts = []
    for s in range(n_species):
        resistance = bath_share / binary[s, n_species]
        for j in range(n_species):
            if j != s:
                resistance = resistance + species[:, j] / binary[s, j]
        mixture = (1.0 - species[:, s]) / resistance
        source_parts.append((species[:, s] + (mixture - dref[s]) * laplacian[:, s]) / dref[s])
    return jnp.stack(source_parts, axis=1)


def block_inverse(values, kron_basis, inverse_diag):
    n_nodes = values.shape[0]
    inner_part = (
        jnp.dot(kron_basis.T, values.reshape(n_nodes, -1), precision=highest).reshape(values.shape)
        * inverse_diag
    )
    return jnp.dot(kron_basis, inner_part.reshape(n_nodes, -1), precision=highest).reshape(
        values.shape
    )


def transform_tables(col_mode, col_part, planes):
    plane_ids = jnp.arange(planes, dtype=jnp.int32)
    phase_id = plane_ids[:, None] * col_mode[None, :] % planes
    angles = phase_id.astype(jnp.float32) * (two_pi / planes)
    trig_table = jnp.where(col_part[None, :] == 0, jnp.cos(angles), -jnp.sin(angles))
    weights = jnp.where(col_mode == 0, 1.0, 2.0).astype(jnp.float32)
    return (trig_table / planes, (trig_table * weights[None, :]).T)


def body(species, laplacian, binary, dref, stiff_eig, basis, rounds, adjacency, edge_map):
    per_side = basis.shape[0]
    n_nodes = per_side * per_side
    n_span = lax.axis_size("span")
    n_elem = lax.axis_size("elem")
    planes = species.shape[2] * n_span
    n_modes = planes // 2
    per_device = n_modes // n_span
    half_tile = per_device // 2
    own_count = adjacency.shape[0]
    source = mixture_source(species, laplacian, binary, dref)
    assign = jnp.arange(n_modes, dtype=jnp.int32).reshape(n_span, per_device)
    tile_count = 1
    col_mode = jnp.broadcast_to(
        assign.reshape(n_span, 2, 1, half_tile), (n_span, 2, 2, half_tile)
    ).reshape(planes)
    col_part = jnp.broadcast_to(
        jnp.arange(2, dtype=jnp.int32).reshape(1, 1, 2, 1), (n_span, 2, 2, half_tile)
    ).reshape(planes)
    forward, backward = transform_tables(col_mode, col_part, planes)
    source_swapped = jnp.transpose(source, (0, 1, 3, 2))
    coeffs = jnp.einsum(
        "nsez,zr->nser",
        lax.all_to_all(source_swapped, "span", split_axis=2, concat_axis=3, tiled=True),
        forward,
        precision=highest,
    )
    exchanged = lax.all_to_all(coeffs, "span", split_axis=3, concat_axis=2, tiled=True)
    modal_rhs = jnp.transpose(exchanged, (0, 1, 3, 2))
    columns = 2 * per_device
    my_modes = lax.dynamic_slice_in_dim(col_mode, lax.axis_index("span") * columns, columns)
    my_rounds = rounds[my_modes]
    wavenumber = my_modes.astype(jnp.float32) * (8.0 / planes)
    shifts = 1.0 / dref[:, None] + (wavenumber * wavenumber)[None, :]
    eig_sum = (stiff_eig[:, None] + stiff_eig[None, :]).reshape(n_nodes)
    inverse_diag = 1.0 / (shifts[None, :, :, None] + eig_sum[:, None, None, None])
    kron_basis = (basis[:, None, :, None] * basis[None, :, None, :]).reshape(n_nodes, n_nodes)
    flat_index = np.array(edge_lists(per_side)).reshape(-1)
    scatter_table = jnp.asarray(edge_matrix(per_side))
    owners = adjacency // own_count
    offset = (owners - lax.axis_index("elem") + n_elem) % n_elem
    local_id = adjacency % own_count
    flat_adj = adjacency.reshape(-1)
    flat_offset = offset.reshape(-1)
    earlier = flat_adj[None, :] < flat_adj[:, None]
    from_prev = flat_offset == n_elem - 1
    from_next = flat_offset == 1
    rank_prev = jnp.sum((earlier & from_prev[None, :]).astype(jnp.int32), axis=1)
    rank_next = jnp.sum((earlier & from_next[None, :]).astype(jnp.int32), axis=1)
    position = jnp.where(
        from_prev,
        own_count + rank_prev,
        jnp.where(from_next, own_count + MESH_X + rank_next, local_id.reshape(-1)),
    ).reshape(adjacency.shape)
    slot_ids = jnp.arange(MESH_X, dtype=jnp.int32)
    faces_next = jnp.any(offset == 1, axis=1)
    faces_prev = jnp.any(offset == n_elem - 1, axis=1)
    slot_next = jnp.cumsum(faces_next.astype(jnp.int32)) - 1
    slot_prev = jnp.cumsum(faces_prev.astype(jnp.int32)) - 1
    pick_next = (faces_next[:, None] & (slot_next[:, None] == slot_ids[None, :])).astype(
        jnp.float32
    )
    pick_prev = (faces_prev[:, None] & (slot_prev[:, None] == slot_ids[None, :])).astype(
        jnp.float32
    )

    def gather_pool(traces):
        send_up = jnp.einsum("ktsce,ea->ktsca", traces, pick_next, precision=highest)
        send_down = jnp.einsum("ktsce,ea->ktsca", traces, pick_prev, precision=highest)
        from_before = from_behind(send_up, "elem", 1)
        from_after = from_behind(send_down, "elem", -1)
        return jnp.concatenate([traces, from_before, from_after], axis=4)

    def couple(modal_field):
        traces = modal_field[flat_index].reshape((4, per_side) + modal_field.shape[1:])
        across = gather_pool(traces)[edge_map, :, :, :, position][:, :, ::-1]
        return jnp.einsum("jtn,ejtsc->nsce", scatter_table, across, precision=highest)

    tile_modes = assign.reshape(n_span, tile_count, per_device // tile_count)
    sweep_bound = jnp.max(rounds[tile_modes[:, 0].reshape(-1)])
    initial = block_inverse(modal_rhs, kron_basis, inverse_diag)

    def sweep_once(sweep_id, modal_field):
        proposal = block_inverse(
            modal_rhs + coupling * couple(modal_field), kron_basis, inverse_diag
        )
        return jnp.where(sweep_id < my_rounds[:, None], proposal, modal_field)

    solved = lax.fori_loop(1, sweep_bound, sweep_once, initial)
    solution_swapped = jnp.transpose(solved, (0, 1, 3, 2))
    values = jnp.einsum(
        "nser,rz->nsez",
        lax.all_to_all(solution_swapped, "span", split_axis=2, concat_axis=3, tiled=True),
        backward,
        precision=highest,
    )
    returned = lax.all_to_all(values, "span", split_axis=3, concat_axis=2, tiled=True)
    return jnp.transpose(returned, (0, 1, 3, 2))


def solution(mesh):
    n_span, n_elem = mesh.shape["span"], mesh.shape["elem"]

    def chosen_body(species, *rest):
        zl, own = species.shape[2:]
        by_rows = n_span * MESH_X == own and 2 * zl == LANES == own and n_elem > 2
        by_rows = by_rows and species.shape[0] == SIDE * SIDE
        return (row_body if by_rows else body)(species, *rest)

    return jax.shard_map(
        chosen_body,
        mesh=mesh,
        in_specs=(
            P(None, None, "span", "elem"),
            P(None, None, "span", "elem"),
            P(),
            P(),
            P(),
            P(),
            P(),
            P("elem", None),
            P("elem", None),
        ),
        out_specs=P(None, None, "span", "elem"),
        check_vma=False,
    )
```

profile of v0, /device:TPU:0, one launch (start us, length us, event | category | flops | bytes accessed | tf_op | source)
XLA Modules:
  0.0 435.2 jit_solution(4682001488486732172)
XLA Ops:
  0.0 2.5 mesh_tables.1
  2.5 7.8 %packed_source.5 = (f32[8,648,128]{2,1,0:T(8,128)}, f32[8,128]{1,0:T(8,128)}) custom-call(f32[3,4]{1,0:T(4,128)} %binary_ref.9, f32[3]{0:T(128)} %dref_ref.9, f32[81,3,64,128]{3,2,1,0:T(8,128)} %species_ref.9, f32[81,3,64,128]{3,2,1,0:T(8,128)} %lap_ref.9, bf16[128,256]{1,0:T(8,128)(2,1)} %get-tuple-element.80.perm_ref), custom_call_target="tpu_custom_call" | custom-call | flops 23000000512 | tf_op jit(solution)/shard_map/packed_source/pallas_call | solution.py:319
  10.3 7.3 %all-to-all-start = ((f32[8,648,128]{2,1,0:T(8,128)}), f32[8,648,128]{2,1,0:T(8,128)S(1)}, u32[]{:S(2)}, u32[]{:S(2)}) async-start(f32[8,648,128]{2,1,0:T(8,128)} %released.10), calls=%async_computation | async-start | bytes 5308416 | tf_op jit(solution)/shard_map/all_to_all | solution.py:701
  17.6 3.5 packed_source.6
  23.8 0.7 copy.49.refs_5_.refs_6_
  25.4 0.8 copy.38.refs_4_.refs_5_
  26.2 5.3 %packed_source.7 = (f32[8,392,128]{2,1,0:T(8,128)}, f32[8,128]{1,0:T(8,128)}) custom-call(f32[3,4]{1,0:T(4,128)} %binary_ref.9, f32[3]{0:T(128)} %dref_ref.9, f32[81,3,64,128]{3,2,1,0:T(8,128)} %species_ref.9, f32[81,3,64,128]{3,2,1,0:T(8,128)} %lap_ref.9, bf16[128,256]{1,0:T(8,128)(2,1)} %get-tuple-element.80.perm_ref, f32[8,128]{1,0:T(8,128)} %get-tuple-element.82.refs_0_), custom_call_target="tpu_custom_call" | custom-call | flops 23000000512 | tf_op jit(solution)/shard_map/packed_source/pallas_call | solution.py:319
  31.6 3.5 packed_source.8
  35.1 5.4 %packed_source.9 = (f32[8,392,128]{2,1,0:T(8,128)}, f32[8,128]{1,0:T(8,128)}) custom-call(f32[3,4]{1,0:T(4,128)} %binary_ref.9, f32[3]{0:T(128)} %dref_ref.9, f32[81,3,64,128]{3,2,1,0:T(8,128)} %species_ref.9, f32[81,3,64,128]{3,2,1,0:T(8,128)} %lap_ref.9, bf16[128,256]{1,0:T(8,128)(2,1)} %get-tuple-element.80.perm_ref, f32[8,128]{1,0:T(8,128)} %get-tuple-element.86.refs_0_), custom_call_target="tpu_custom_call" | custom-call | flops 23000000512 | tf_op jit(solution)/shard_map/packed_source/pallas_call | solution.py:319
  41.4 1.1 slice_bitcast_fusion
  42.5 3.6 link_matrices.1
  46.1 31.6 %all-to-all-done.refs_0_.refs_8_ = f32[8,648,128]{2,1,0:T(8,128)S(1)} async-done(((f32[8,648,128]{2,1,0:T(8,128)}), f32[8,648,128]{2,1,0:T(8,128)S(1)}, u32[]{:S(2)}, u32[]{:S(2)}) %all-to-all-start) | async-done | bytes 2654240 | tf_op jit(solution)/shard_map/all_to_all | solution.py:701
  77.7 4.2 all-to-all-start.1
  82.0 10.5 %start_solve.3 = (f32[1408,512]{1,0:T(8,128)}, f32[640,512]{1,0:T(8,128)}, f32[144,512]{1,0:T(8,128)}, f32[144,512]{1,0:T(8,128)}, f32[8,128]{1,0:T(8,128)}) custom-call(f32[8,648,128]{2,1,0:T(8,128)} %copy-done.7, bf16[512,512]{1,0:T(8,128)(2,1)} %constant.50.clone.refs_1_.refs_2_, bf16[512,512]{1,0:T(8,128)(2,1)} %constant.51.clone.refs_2_.refs_3_, ...), custom_call_target="tpu_custom_call" | custom-call | flops 92000002048 | tf_op jit(solution)/shard_map/start_solve/pallas_call | solution.py:577
  92.7 1.8 collective-permute-start.1
  95.8 11.7 %all-to-all-done.1.refs_11_.refs_0_ = f32[8,256,128]{2,1,0:T(8,128)} async-done(((f32[8,256,128]{2,1,0:T(8,128)}), f32[8,256,128]{2,1,0:T(8,128)}, u32[]{:S(2)}, u32[]{:S(2)}) %all-to-all-start.1) | async-done | bytes 1048608 | tf_op jit(solution)/shard_map/all_to_all | solution.py:701
  107.6 4.1 all-to-all-start.3
  111.7 0.7 copy-done.23
  112.5 8.1 %sweep_solve.6 = (f32[640,512]{1,0:T(8,128)}, f32[640,512]{1,0:T(8,128)}, f32[144,512]{1,0:T(8,128)}, f32[144,512]{1,0:T(8,128)}, f32[8,128]{1,0:T(8,128)}) custom-call(s32[1,512]{1,0:T(1,128)} %bitcast.20, f32[176,512]{1,0:T(8,128)} %get-tuple-element.146.refs_3_.refs_1_, bf16[640,928]{1,0:T(8,128)(2,1)} %get-tuple-element.78.refs_2_, ...), custom_call_target="tpu_custom_call" | custom-call | flops 57500000256 | tf_op jit(solution)/shard_map/sweep_solve/pallas_call | solution.py:577
  120.6 0.7 collective-permute-start.2
  121.3 1.6 collective-permute-start.3
  123.0 0.7 pad_maximum_fusion.refs_4_
  123.7 25.6 %all-to-all-done.3.refs_12_.refs_1_.refs_9_ = f32[8,392,128]{2,1,0:T(8,128)S(1)} async-done(((f32[8,392,128]{2,1,0:T(8,128)}), f32[8,392,128]{2,1,0:T(8,128)S(1)}, u32[]{:S(2)}, u32[]{:S(2)}) %all-to-all-start.3) | async-done | bytes 1605664 | tf_op jit(solution)/shard_map/all_to_all | solution.py:701
  149.3 4.6 %all-to-all-start.2 = ((f32[8,256,128]{2,1,0:T(8,128)}), f32[8,256,128]{2,1,0:T(8,128)}, u32[]{:S(2)}, u32[]{:S(2)}) async-start(f32[8,256,128]{2,1,0:T(8,128)} %released.12), calls=%async_computation.2 | async-start | bytes 2097152 | tf_op jit(solution)/shard_map/all_to_all | solution.py:701
  154.8 8.5 %sweep_solve.7 = (f32[640,512]{1,0:T(8,128)}, f32[640,512]{1,0:T(8,128)}, f32[144,512]{1,0:T(8,128)}, f32[144,512]{1,0:T(8,128)}, f32[8,128]{1,0:T(8,128)}) custom-call(s32[1,512]{1,0:T(1,128)} %bitcast.21, f32[176,512]{1,0:T(8,128)} %get-tuple-element.146.refs_3_.refs_1_, bf16[640,928]{1,0:T(8,128)(2,1)} %get-tuple-element.78.refs_2_, ...), custom_call_target="tpu_custom_call" | custom-call | flops 57500000256 | tf_op jit(solution)/shard_map/sweep_solve/pallas_call | solution.py:577
  163.3 0.8 collective-permute-start.6
  164.1 1.3 collective-permute-start.7
  165.4 10.0 %start_solve.4 = (f32[1408,512]{1,0:T(8,128)}, f32[640,512]{1,0:T(8,128)}, f32[144,512]{1,0:T(8,128)}, f32[144,512]{1,0:T(8,128)}, f32[8,128]{1,0:T(8,128)}) custom-call(f32[8,256,128]{2,1,0:T(8,128)} %all-to-all-done.1.refs_11_.refs_0_, f32[8,392,128]{2,1,0:T(8,128)} %copy-done.8, bf16[512,512]{1,0:T(8,128)(2,1)} %constant.50.clone.refs_1_.refs_2_, ...), custom_call_target="tpu_custom_call" | custom-call | flops 92000002048 | tf_op jit(solution)/shard_map/start_solve/pallas_call | solution.py:577
  175.8 1.6 collective-permute-start.5
  177.4 2.5 all-to-all-done.2.refs_13_.refs_11_.refs_0_
  179.9 4.5 %all-to-all-start.4 = ((f32[8,392,128]{2,1,0:T(8,128)}), f32[8,392,128]{2,1,0:T(8,128)}, u32[]{:S(2)}, u32[]{:S(2)}) async-start(f32[8,392,128]{2,1,0:T(8,128)} %released.14), calls=%async_computation.4 | async-start | bytes 3211264 | tf_op jit(solution)/shard_map/all_to_all | solution.py:701
  185.2 12.5 %finish_solve.3 = (f32[8,256,128]{2,1,0:T(8,128)}, f32[8,392,128]{2,1,0:T(8,128)}, f32[8,128]{1,0:T(8,128)}) custom-call(s32[1,512]{1,0:T(1,128)} %bitcast.22, f32[176,512]{1,0:T(8,128)} %get-tuple-element.146.refs_3_.refs_1_, bf16[640,928]{1,0:T(8,128)(2,1)} %get-tuple-element.78.refs_2_, bf16[352,80]{1,0:T(8,128)(2,1)} %pad_maximum_fusion.2.refs_4_.refs_3_, ...), custom_call_target="tpu_custom_call" | custom-call | flops 97749999616 | tf_op jit(solution)/shard_map/finish_solve/pallas_call | solution.py:577
  198.6 8.1 %sweep_solve.8 = (f32[640,512]{1,0:T(8,128)}, f32[640,512]{1,0:T(8,128)}, f32[144,512]{1,0:T(8,128)}, f32[144,512]{1,0:T(8,128)}, f32[8,128]{1,0:T(8,128)}) custom-call(s32[1,512]{1,0:T(1,128)} %bitcast.23, f32[176,512]{1,0:T(8,128)} %get-tuple-element.145.refs_4_.refs_1_, bf16[640,928]{1,0:T(8,128)(2,1)} %get-tuple-element.78.refs_2_, ...), custom_call_target="tpu_custom_call" | custom-call | flops 57500000256 | tf_op jit(solution)/shard_map/sweep_solve/pallas_call | solution.py:577
  207.2 2.0 collective-permute-start.9
  209.2 12.9 %all-to-all-done.4.refs_12_.refs_1_.refs_9_ = f32[8,392,128]{2,1,0:T(8,128)} async-done(((f32[8,392,128]{2,1,0:T(8,128)}), f32[8,392,128]{2,1,0:T(8,128)}, u32[]{:S(2)}, u32[]{:S(2)}) %all-to-all-start.4) | async-done | bytes 1605664 | tf_op jit(solution)/shard_map/all_to_all | solution.py:701
  222.1 4.3 all-to-all-start.5
  226.4 0.7 copy-done.30
  227.2 8.5 %sweep_solve.9 = (f32[640,512]{1,0:T(8,128)}, f32[640,512]{1,0:T(8,128)}, f32[144,512]{1,0:T(8,128)}, f32[144,512]{1,0:T(8,128)}, f32[8,128]{1,0:T(8,128)}) custom-call(s32[1,512]{1,0:T(1,128)} %bitcast.24, f32[176,512]{1,0:T(8,128)} %get-tuple-element.145.refs_4_.refs_1_, bf16[640,928]{1,0:T(8,128)(2,1)} %get-tuple-element.78.refs_2_, ...), custom_call_target="tpu_custom_call" | custom-call | flops 57500000256 | tf_op jit(solution)/shard_map/sweep_solve/pallas_call | solution.py:577
  236.1 2.3 collective-permute-start.13
  238.4 9.9 %start_solve.5 = (f32[1408,512]{1,0:T(8,128)}, f32[640,512]{1,0:T(8,128)}, f32[144,512]{1,0:T(8,128)}, f32[144,512]{1,0:T(8,128)}, f32[8,128]{1,0:T(8,128)}) custom-call(f32[8,256,128]{2,1,0:T(8,128)} %all-to-all-done.2.refs_13_.refs_11_.refs_0_, f32[8,392,128]{2,1,0:T(8,128)} %all-to-all-done.4.refs_12_.refs_1_.refs_9_, ...), custom_call_target="tpu_custom_call" | custom-call | flops 92000002048 | tf_op jit(solution)/shard_map/start_solve/pallas_call | solution.py:577
  248.3 2.0 collective-permute-start.11
  250.4 1.7 all-to-all-done.5.refs_13_.refs_11_.recv_ref
  252.1 4.3 all-to-all-start.6
  257.2 12.6 %finish_solve.4 = (f32[8,256,128]{2,1,0:T(8,128)}, f32[8,392,128]{2,1,0:T(8,128)}, f32[8,128]{1,0:T(8,128)}) custom-call(s32[1,512]{1,0:T(1,128)} %bitcast.25, f32[176,512]{1,0:T(8,128)} %get-tuple-element.145.refs_4_.refs_1_, bf16[640,928]{1,0:T(8,128)(2,1)} %get-tuple-element.78.refs_2_, bf16[352,80]{1,0:T(8,128)(2,1)} %pad_maximum_fusion.2.refs_4_.refs_3_, ...), custom_call_target="tpu_custom_call" | custom-call | flops 97749999616 | tf_op jit(solution)/shard_map/finish_solve/pallas_call | solution.py:577
  270.6 8.1 %sweep_solve.10 = (f32[640,512]{1,0:T(8,128)}, f32[640,512]{1,0:T(8,128)}, f32[144,512]{1,0:T(8,128)}, f32[144,512]{1,0:T(8,128)}, f32[8,128]{1,0:T(8,128)}) custom-call(s32[1,512]{1,0:T(1,128)} %bitcast.26, f32[176,512]{1,0:T(8,128)} %get-tuple-element.147.refs_4_.refs_1_, bf16[640,928]{1,0:T(8,128)(2,1)} %get-tuple-element.78.refs_2_, ...), custom_call_target="tpu_custom_call" | custom-call | flops 57500000256 | tf_op jit(solution)/shard_map/sweep_solve/pallas_call | solution.py:577
  278.7 2.5 collective-permute-start.15
  281.2 12.3 %all-to-all-done.6.refs_12_.recv_ref = f32[8,392,128]{2,1,0:T(8,128)} async-done(((f32[8,392,128]{2,1,0:T(8,128)}), f32[8,392,128]{2,1,0:T(8,128)}, u32[]{:S(2)}, u32[]{:S(2)}) %all-to-all-start.6) | async-done | bytes 1605664 | tf_op jit(solution)/shard_map/all_to_all | solution.py:701
  293.5 4.5 %all-to-all-start.7 = ((f32[8,256,128]{2,1,0:T(8,128)}), f32[8,256,128]{2,1,0:T(8,128)S(1)}, u32[]{:S(2)}, u32[]{:S(2)}) async-start(f32[8,256,128]{2,1,0:T(8,128)} %released.17), calls=%async_computation.7 | async-start | bytes 2097152 | tf_op jit(solution)/shard_map/all_to_all | solution.py:701
  298.1 0.7 copy-done.29
  298.9 8.5 %sweep_solve.11 = (f32[640,512]{1,0:T(8,128)}, f32[640,512]{1,0:T(8,128)}, f32[144,512]{1,0:T(8,128)}, f32[144,512]{1,0:T(8,128)}, f32[8,128]{1,0:T(8,128)}) custom-call(s32[1,512]{1,0:T(1,128)} %bitcast.27, f32[176,512]{1,0:T(8,128)} %get-tuple-element.147.refs_4_.refs_1_, bf16[640,928]{1,0:T(8,128)(2,1)} %get-tuple-element.78.refs_2_, ...), custom_call_target="tpu_custom_call" | custom-call | flops 57500000256 | tf_op jit(solution)/shard_map/sweep_solve/pallas_call | solution.py:577
  307.5 2.2 collective-permute-start.17
  309.6 13.7 %all-to-all-done.7.refs_13_.recv_ref = f32[8,256,128]{2,1,0:T(8,128)S(1)} async-done(((f32[8,256,128]{2,1,0:T(8,128)}), f32[8,256,128]{2,1,0:T(8,128)S(1)}, u32[]{:S(2)}, u32[]{:S(2)}) %all-to-all-start.7) | async-done | bytes 1048608 | tf_op jit(solution)/shard_map/all_to_all | solution.py:701
  323.4 1.0 copy-done.4
  324.3 3.6 all-to-all-start.8
  328.8 12.9 %finish_solve.5 = (f32[8,648,128]{2,1,0:T(8,128)}, f32[8,128]{1,0:T(8,128)}) custom-call(s32[1,512]{1,0:T(1,128)} %bitcast.28, f32[176,512]{1,0:T(8,128)} %get-tuple-element.147.refs_4_.refs_1_, bf16[640,928]{1,0:T(8,128)(2,1)} %get-tuple-element.78.refs_2_, bf16[352,80]{1,0:T(8,128)(2,1)} %pad_maximum_fusion.2.refs_4_.refs_3_, ...), custom_call_target="tpu_custom_call" | custom-call | flops 97749999616 | tf_op jit(solution)/shard_map/finish_solve/pallas_call | solution.py:577
  341.7 23.9 %all-to-all-done.8.refs_2_.recv_ref = f32[8,392,128]{2,1,0:T(8,128)S(1)} async-done(((f32[8,392,128]{2,1,0:T(8,128)}), f32[8,392,128]{2,1,0:T(8,128)S(1)}, u32[]{:S(2)}, u32[]{:S(2)}) %all-to-all-start.8) | async-done | bytes 1605664 | tf_op jit(solution)/shard_map/all_to_all | solution.py:701
  365.6 1.2 copy-done.2
  366.8 3.8 all-to-all-start.9
  370.6 2.6 unpacked.5.refs_0_
  373.2 4.1 unpacked.6.refs_0_
  377.2 1.6 unpacked.7.refs_0_
  378.8 2.6 unpacked.8.refs_0_
  381.5 49.4 %all-to-all-done.9.recv_ref = f32[8,648,128]{2,1,0:T(8,128)S(1)} async-done(((f32[8,648,128]{2,1,0:T(8,128)}), f32[8,648,128]{2,1,0:T(8,128)S(1)}, u32[]{:S(2)}, u32[]{:S(2)}) %all-to-all-start.9) | async-done | bytes 2654240 | tf_op jit(solution)/shard_map/all_to_all | solution.py:701
  430.9 3.8 unpacked.9
  (126 shorter events, 12.7 us)
Async XLA Ops:
  0.0 94.5 %copy-start = (s32[256]{0:T(256)S(1)}, s32[256]{0:T(256)}, u32[]{:S(2)}) copy-start(s32[256]{0:T(256)} %param.28) | copy-start | bytes 3076
  10.3 67.4 %all-to-all-start = ((f32[8,648,128]{2,1,0:T(8,128)}), f32[8,648,128]{2,1,0:T(8,128)S(1)}, u32[]{:S(2)}, u32[]{:S(2)}) async-start(f32[8,648,128]{2,1,0:T(8,128)} %released.10), calls=%async_computation | async-start | bytes 5308416 | tf_op jit(solution)/shard_map/all_to_all | solution.py:701
  17.5 3.6 copy-start.13
  17.5 3.6 copy-start.14
  17.6 3.6 copy-start.12
  17.6 3.8 copy-start.11
  40.5 0.7 copy-start.33
  77.7 4.2 copy-start.7
  77.7 29.9 %all-to-all-start.1 = ((f32[8,256,128]{2,1,0:T(8,128)}), f32[8,256,128]{2,1,0:T(8,128)}, u32[]{:S(2)}, u32[]{:S(2)}) async-start(f32[8,256,128]{2,1,0:T(8,128)} %released.11), calls=%async_computation.1 | async-start | bytes 2097152 | tf_op jit(solution)/shard_map/all_to_all | solution.py:701
  82.0 13.1 %copy-start.10 = (f32[88,40]{1,0:T(8,128)S(1)}, f32[88,40]{1,0:T(8,128)}, u32[]{:S(2)}) copy-start(f32[88,40]{1,0:T(8,128)} %get-tuple-element.155) | copy-start | bytes 42244
  92.5 19.2 %collective-permute-start = (f32[144,512]{1,0:T(8,128)}, f32[144,512]{1,0:T(8,128)S(1)}, u32[]{:S(2)}, u32[]{:S(2)}) collective-permute-start(f32[144,512]{1,0:T(8,128)} %get-tuple-element.89), channel_id=1, source_target_pairs={{0,3},{4,0},{12,4},{8,12},{16,8},{20,16},{28,20},{24,28},{25,24},{... | collective-permute-start | bytes 884744 | tf_op jit(solution)/shard_map/ppermute | solution.py:631
  92.7 19.0 %collective-permute-start.1 = (f32[144,512]{1,0:T(8,128)}, f32[144,512]{1,0:T(8,128)S(1)}, u32[]{:S(2)}, u32[]{:S(2)}) collective-permute-start(f32[144,512]{1,0:T(8,128)} %get-tuple-element.90), channel_id=1, source_target_pairs={{0,4},{4,12},{12,8},{8,16},{16,20},{20,28},{28,24},{24,25},{25,29}... | collective-permute-start | bytes 884744 | tf_op jit(solution)/shard_map/ppermute | solution.py:630
  107.6 41.7 %all-to-all-start.3 = ((f32[8,392,128]{2,1,0:T(8,128)}), f32[8,392,128]{2,1,0:T(8,128)S(1)}, u32[]{:S(2)}, u32[]{:S(2)}) async-start(f32[8,392,128]{2,1,0:T(8,128)} %released.13), calls=%async_computation.3 | async-start | bytes 3211264 | tf_op jit(solution)/shard_map/all_to_all | solution.py:701
  111.7 0.7 copy-start.23
  111.7 0.8 copy-start.25
  112.5 10.4 %copy-start.9 = (f32[88,88]{1,0:T(8,128)S(1)}, f32[88,88]{1,0:T(8,128)}, u32[]{:S(2)}) copy-start(f32[88,88]{1,0:T(8,128)} %get-tuple-element.151) | copy-start | bytes 92932
  120.6 33.4 %collective-permute-start.2 = (f32[144,512]{1,0:T(8,128)}, f32[144,512]{1,0:T(8,128)S(1)}, u32[]{:S(2)}, u32[]{:S(2)}) collective-permute-start(f32[144,512]{1,0:T(8,128)} %get-tuple-element.97), channel_id=1, source_target_pairs={{0,3},{4,0},{12,4},{8,12},{16,8},{20,16},{28,20},{24,28},{25,24},{... | collective-permute-start | bytes 884744 | tf_op jit(solution)/shard_map/ppermute | solution.py:631
  121.3 32.7 %collective-permute-start.3 = (f32[144,512]{1,0:T(8,128)}, f32[144,512]{1,0:T(8,128)S(1)}, u32[]{:S(2)}, u32[]{:S(2)}) collective-permute-start(f32[144,512]{1,0:T(8,128)} %get-tuple-element.98), channel_id=1, source_target_pairs={{0,4},{4,12},{12,8},{8,16},{16,20},{20,28},{28,24},{24,25},{25,29}... | collective-permute-start | bytes 884744 | tf_op jit(solution)/shard_map/ppermute | solution.py:630
  149.3 4.7 %copy-start.8 = (f32[8,392,128]{2,1,0:T(8,128)}, f32[8,392,128]{2,1,0:T(8,128)S(1)}, u32[]{:S(2)}) copy-start(f32[8,392,128]{2,1,0:T(8,128)S(1)} %all-to-all-done.3.refs_12_.refs_1_.refs_9_) | copy-start | bytes 4816900
  149.3 30.6 %all-to-all-start.2 = ((f32[8,256,128]{2,1,0:T(8,128)}), f32[8,256,128]{2,1,0:T(8,128)}, u32[]{:S(2)}, u32[]{:S(2)}) async-start(f32[8,256,128]{2,1,0:T(8,128)} %released.12), calls=%async_computation.2 | async-start | bytes 2097152 | tf_op jit(solution)/shard_map/all_to_all | solution.py:701
  154.0 0.7 copy-start.24
  154.0 0.8 copy-start.26
  163.3 21.1 %collective-permute-start.6 = (f32[144,512]{1,0:T(8,128)}, f32[144,512]{1,0:T(8,128)S(1)}, u32[]{:S(2)}, u32[]{:S(2)}) collective-permute-start(f32[144,512]{1,0:T(8,128)} %get-tuple-element.106), channel_id=1, source_target_pairs={{0,3},{4,0},{12,4},{8,12},{16,8},{20,16},{28,20},{24,28},{25,24},{... | collective-permute-start | bytes 884744 | tf_op jit(solution)/shard_map/ppermute | solution.py:631
  164.1 20.3 %collective-permute-start.7 = (f32[144,512]{1,0:T(8,128)}, f32[144,512]{1,0:T(8,128)S(1)}, u32[]{:S(2)}, u32[]{:S(2)}) collective-permute-start(f32[144,512]{1,0:T(8,128)} %get-tuple-element.107), channel_id=1, source_target_pairs={{0,4},{4,12},{12,8},{8,16},{16,20},{20,28},{28,24},{24,25},{25,29}... | collective-permute-start | bytes 884744 | tf_op jit(solution)/shard_map/ppermute | solution.py:630
  175.4 22.4 %collective-permute-start.4 = (f32[144,512]{1,0:T(8,128)}, f32[144,512]{1,0:T(8,128)S(1)}, u32[]{:S(2)}, u32[]{:S(2)}) collective-permute-start(f32[144,512]{1,0:T(8,128)} %get-tuple-element.103), channel_id=1, source_target_pairs={{0,3},{4,0},{12,4},{8,12},{16,8},{20,16},{28,20},{24,28},{25,24},{... | collective-permute-start | bytes 884744 | tf_op jit(solution)/shard_map/ppermute | solution.py:631
  175.8 22.0 %collective-permute-start.5 = (f32[144,512]{1,0:T(8,128)}, f32[144,512]{1,0:T(8,128)S(1)}, u32[]{:S(2)}, u32[]{:S(2)}) collective-permute-start(f32[144,512]{1,0:T(8,128)} %get-tuple-element.104), channel_id=1, source_target_pairs={{0,4},{4,12},{12,8},{8,16},{16,20},{20,28},{28,24},{24,25},{25,29}... | collective-permute-start | bytes 884744 | tf_op jit(solution)/shard_map/ppermute | solution.py:630
  179.9 42.1 %all-to-all-start.4 = ((f32[8,392,128]{2,1,0:T(8,128)}), f32[8,392,128]{2,1,0:T(8,128)}, u32[]{:S(2)}, u32[]{:S(2)}) async-start(f32[8,392,128]{2,1,0:T(8,128)} %released.14), calls=%async_computation.4 | async-start | bytes 3211264 | tf_op jit(solution)/shard_map/all_to_all | solution.py:701
  184.4 0.7 copy-start.17
  184.4 0.8 copy-start.20
  197.8 0.7 copy-start.18
  197.8 0.8 copy-start.21
  206.7 19.6 %collective-permute-start.8 = (f32[144,512]{1,0:T(8,128)}, f32[144,512]{1,0:T(8,128)S(1)}, u32[]{:S(2)}, u32[]{:S(2)}) collective-permute-start(f32[144,512]{1,0:T(8,128)} %get-tuple-element.112), channel_id=1, source_target_pairs={{0,3},{4,0},{12,4},{8,12},{16,8},{20,16},{28,20},{24,28},{25,24},{... | collective-permute-start | bytes 884744 | tf_op jit(solution)/shard_map/ppermute | solution.py:631
  207.2 19.1 %collective-permute-start.9 = (f32[144,512]{1,0:T(8,128)}, f32[144,512]{1,0:T(8,128)S(1)}, u32[]{:S(2)}, u32[]{:S(2)}) collective-permute-start(f32[144,512]{1,0:T(8,128)} %get-tuple-element.113), channel_id=1, source_target_pairs={{0,4},{4,12},{12,8},{8,16},{16,20},{20,28},{28,24},{24,25},{25,29}... | collective-permute-start | bytes 884744 | tf_op jit(solution)/shard_map/ppermute | solution.py:630
  222.1 30.0 %all-to-all-start.5 = ((f32[8,256,128]{2,1,0:T(8,128)}), f32[8,256,128]{2,1,0:T(8,128)}, u32[]{:S(2)}, u32[]{:S(2)}) async-start(f32[8,256,128]{2,1,0:T(8,128)} %released.15), calls=%async_computation.5 | async-start | bytes 2097152 | tf_op jit(solution)/shard_map/all_to_all | solution.py:701
  226.3 0.7 copy-start.30
  226.4 0.8 copy-start.32
  235.7 20.6 %collective-permute-start.12 = (f32[144,512]{1,0:T(8,128)}, f32[144,512]{1,0:T(8,128)S(1)}, u32[]{:S(2)}, u32[]{:S(2)}) collective-permute-start(f32[144,512]{1,0:T(8,128)} %get-tuple-element.121), channel_id=1, source_target_pairs={{0,3},{4,0},{12,4},{8,12},{16,8},{20,16},{28,20},{24,28},{25,24},{... | collective-permute-start | bytes 884744 | tf_op jit(solution)/shard_map/ppermute | solution.py:631
  236.1 20.3 %collective-permute-start.13 = (f32[144,512]{1,0:T(8,128)}, f32[144,512]{1,0:T(8,128)S(1)}, u32[]{:S(2)}, u32[]{:S(2)}) collective-permute-start(f32[144,512]{1,0:T(8,128)} %get-tuple-element.122), channel_id=1, source_target_pairs={{0,4},{4,12},{12,8},{8,16},{16,20},{20,28},{28,24},{24,25},{25,29}... | collective-permute-start | bytes 884744 | tf_op jit(solution)/shard_map/ppermute | solution.py:630
  248.3 21.5 %collective-permute-start.10 = (f32[144,512]{1,0:T(8,128)}, f32[144,512]{1,0:T(8,128)S(1)}, u32[]{:S(2)}, u32[]{:S(2)}) collective-permute-start(f32[144,512]{1,0:T(8,128)} %get-tuple-element.118), channel_id=1, source_target_pairs={{0,3},{4,0},{12,4},{8,12},{16,8},{20,16},{28,20},{24,28},{25,24},{... | collective-permute-start | bytes 884744 | tf_op jit(solution)/shard_map/ppermute | solution.py:631
  248.3 21.5 %collective-permute-start.11 = (f32[144,512]{1,0:T(8,128)}, f32[144,512]{1,0:T(8,128)S(1)}, u32[]{:S(2)}, u32[]{:S(2)}) collective-permute-start(f32[144,512]{1,0:T(8,128)} %get-tuple-element.119), channel_id=1, source_target_pairs={{0,4},{4,12},{12,8},{8,16},{16,20},{20,28},{28,24},{24,25},{25,29}... | collective-permute-start | bytes 884744 | tf_op jit(solution)/shard_map/ppermute | solution.py:630
  252.1 41.5 %all-to-all-start.6 = ((f32[8,392,128]{2,1,0:T(8,128)}), f32[8,392,128]{2,1,0:T(8,128)}, u32[]{:S(2)}, u32[]{:S(2)}) async-start(f32[8,392,128]{2,1,0:T(8,128)} %released.16), calls=%async_computation.6 | async-start | bytes 3211264 | tf_op jit(solution)/shard_map/all_to_all | solution.py:701
  256.4 0.7 copy-start.15
  256.4 0.8 copy-start.16
  269.8 0.7 copy-start.19
  269.9 0.7 copy-start.22
  278.7 19.3 %collective-permute-start.14 = (f32[144,512]{1,0:T(8,128)}, f32[144,512]{1,0:T(8,128)S(1)}, u32[]{:S(2)}, u32[]{:S(2)}) collective-permute-start(f32[144,512]{1,0:T(8,128)} %get-tuple-element.129), channel_id=1, source_target_pairs={{0,3},{4,0},{12,4},{8,12},{16,8},{20,16},{28,20},{24,28},{25,24},{... | collective-permute-start | bytes 884744 | tf_op jit(solution)/shard_map/ppermute | solution.py:631
  278.7 19.3 %collective-permute-start.15 = (f32[144,512]{1,0:T(8,128)}, f32[144,512]{1,0:T(8,128)S(1)}, u32[]{:S(2)}, u32[]{:S(2)}) collective-permute-start(f32[144,512]{1,0:T(8,128)} %get-tuple-element.130), channel_id=1, source_target_pairs={{0,4},{4,12},{12,8},{8,16},{16,20},{20,28},{28,24},{24,25},{25,29}... | collective-permute-start | bytes 884744 | tf_op jit(solution)/shard_map/ppermute | solution.py:630
  293.5 29.8 %all-to-all-start.7 = ((f32[8,256,128]{2,1,0:T(8,128)}), f32[8,256,128]{2,1,0:T(8,128)S(1)}, u32[]{:S(2)}, u32[]{:S(2)}) async-start(f32[8,256,128]{2,1,0:T(8,128)} %released.17), calls=%async_computation.7 | async-start | bytes 2097152 | tf_op jit(solution)/shard_map/all_to_all | solution.py:701
  298.0 0.7 copy-start.29
  298.1 0.8 copy-start.31
  307.4 20.5 %collective-permute-start.16 = (f32[144,512]{1,0:T(8,128)}, f32[144,512]{1,0:T(8,128)S(1)}, u32[]{:S(2)}, u32[]{:S(2)}) collective-permute-start(f32[144,512]{1,0:T(8,128)} %get-tuple-element.135), channel_id=1, source_target_pairs={{0,3},{4,0},{12,4},{8,12},{16,8},{20,16},{28,20},{24,28},{25,24},{... | collective-permute-start | bytes 884744 | tf_op jit(solution)/shard_map/ppermute | solution.py:631
  307.5 20.5 %collective-permute-start.17 = (f32[144,512]{1,0:T(8,128)}, f32[144,512]{1,0:T(8,128)S(1)}, u32[]{:S(2)}, u32[]{:S(2)}) collective-permute-start(f32[144,512]{1,0:T(8,128)} %get-tuple-element.136), channel_id=1, source_target_pairs={{0,4},{4,12},{12,8},{8,16},{16,20},{20,28},{28,24},{24,25},{25,29}... | collective-permute-start | bytes 884744 | tf_op jit(solution)/shard_map/ppermute | solution.py:630
  323.4 1.0 copy-start.4
  324.3 41.3 %all-to-all-start.8 = ((f32[8,392,128]{2,1,0:T(8,128)}), f32[8,392,128]{2,1,0:T(8,128)S(1)}, u32[]{:S(2)}, u32[]{:S(2)}) async-start(f32[8,392,128]{2,1,0:T(8,128)} %released.18), calls=%async_computation.8 | async-start | bytes 3211264 | tf_op jit(solution)/shard_map/all_to_all | solution.py:701
  327.9 0.7 copy-start.27
  328.0 0.8 copy-start.28
  365.6 1.2 copy-start.2
  366.8 3.8 copy-start.6
  366.8 64.1 %all-to-all-start.9 = ((f32[8,648,128]{2,1,0:T(8,128)}), f32[8,648,128]{2,1,0:T(8,128)S(1)}, u32[]{:S(2)}, u32[]{:S(2)}) async-start(f32[8,648,128]{2,1,0:T(8,128)} %released.19), calls=%async_computation.9 | async-start | bytes 5308416 | tf_op jit(solution)/shard_map/all_to_all | solution.py:701
  373.2 4.1 copy-start.5
  377.2 1.6 copy-start.3
  430.9 3.8 copy-start.1
where the time goes:
time: 444 us; the launch traced here: 435 us
  waiting for transfers between devices  186 us (42%)
  Pallas kernels  165 us (37%)
  starting transfers between devices  65.4 us (15%)
  local copies, waits for them, and re-layouts  15.5 us (3%)
    all_to_all x10, waiting for transfers between devices, across(): return lax.all_to_all(sent, 'span', split_axis=0, concat_axis=0, tiled=True)  185 us
    pallas_call x12, Pallas kernels, vmem_call(): pl.pallas_call(ordered, out_shape=tuple(out_shape) + (DONE,), in_specs=[v...  118 us
    all_to_all x10, starting transfers between devices, across(): return lax.all_to_all(sent, 'span', split_axis=0, concat_axis=0, tiled=True)  45.1 us
    pallas_call x5, Pallas kernels, packed_source(): pl.pallas_call(functools.partial(source_kernel, s, part), grid=(steps,),...  25.5 us
    ppermute x9, starting transfers between devices, exchange(): below = lax.ppermute(up, axes, ring_route(n_span, n_elem, 1))  17.2 us
    pallas_call x5, Pallas kernels, unpacked(): pl.pallas_call(functools.partial(unpack_kernel, part), grid=(steps,), out...  14.7 us
    unnamed x71, local copies, waits for them, and re-layouts  10.6 us
  transfers between devices with their start and end apart: 28, of which 11 were waited for; matrix products, arithmetic and copies ran while one was open for 2% of the time, Pallas kernels for 35%

commit v1 on v0

--- a/solution.py
+++ b/solution.py
@@ -18,7 +18,6 @@
 N_SWEEPS = 3
 WHOLE = 2
 COST_SCALE = 5
-FIRST_WHOLE = True
 DONE = jax.ShapeDtypeStruct((8, LANES), jnp.float32)
 VMEM_BYTES = 60 * 1024 * 1024
 UNPACK_BYTES = 48 * 1024 * 1024
@@ -232,7 +231,7 @@
     )(base, step, send, from_edge, turn, skip, out_edge, move)
 
 
-def source_kernel(s, part, binary_ref, dref_ref, species_ref, lap_ref, perm_ref, *refs):
+def source_kernel(s, part, n_nodes, binary_ref, dref_ref, species_ref, lap_ref, perm_ref, *refs):
     out_ref, done_ref = refs[-2:]
     done_ref[...] = jnp.zeros_like(done_ref)
     per_step, n_species, zl, own = species_ref.shape
@@ -266,22 +265,25 @@
             perm, both, (((1,), (1,)), ((), ())), preferred_element_type=f32
         )
 
-    def blocks():
+    def blocks(count=None):
         pairs = per_step // 2
-        for k in range(pairs):
+        for k in range(pairs if count is None else count):
             tile = turned(source(2 * k), source(2 * k + 1))
             for q in range(n_span):
                 rows = block_rows(part, k, pairs)
                 out_ref[q, rows, :] = tile[q * MESH_X : (q + 1) * MESH_X]
 
     def tail():
-        value = source(0)
+        left = before_tail(n_nodes, per_step)
+        blocks(left // 2)
+        value = source(left)
         tile = turned(value, value)
         half = MESH_X // 2
         low = lax.broadcasted_iota(jnp.int32, (half, 2 * zl), 1) < zl
         for q in range(n_span):
             block = tile[q * MESH_X : (q + 1) * MESH_X]
-            out_ref[q, :half, :] = jnp.where(low, block[:half], block[half:])
+            row = left // 2 * MESH_X
+            out_ref[q, row : row + half, :] = jnp.where(low, block[:half], block[half:])
 
     by_step(part > 0, blocks, tail)
 
@@ -290,6 +292,10 @@
     if part == WHOLE:
         return slice(k * MESH_X, (k + 1) * MESH_X)
     return pl.ds(k, MESH_X, stride=pairs)
+
+
+def before_tail(n_nodes, per_step):
+    return (n_nodes - 1) % per_step
 
 
 def by_step(has_tail, blocks, tail):
@@ -306,18 +312,18 @@
     rows = MESH_X * PAIRS
     first = groups // 2
     if part == 0:
-        return 0, first, first * rows
+        return 0, first, first * rows, PAIRS
     if part == WHOLE:
-        return 0, groups + 1, groups * rows + MESH_X // 2
-    return first, groups - first + 1, (groups - first) * rows + MESH_X // 2
+        return 0, -(-n_nodes // (4 * PAIRS)), groups * rows + MESH_X // 2, 2 * PAIRS
+    return first, groups - first + 1, (groups - first) * rows + MESH_X // 2, PAIRS
 
 
 def packed_source(s, part, species, laplacian, binary, dref, perm, n_span, after):
     n_nodes, n_species, zl, own = species.shape
-    step = 2 * PAIRS
-    begin, steps, rows = part_blocks(n_nodes, part)
+    begin, steps, rows, pairs = part_blocks(n_nodes, part)
+    step = 2 * pairs
     return pl.pallas_call(
-        functools.partial(source_kernel, s, part),
+        functools.partial(source_kernel, s, part, n_nodes),
         grid=(steps,),
         out_shape=(jax.ShapeDtypeStruct((n_span, rows, 2 * zl), f32), DONE),
         in_specs=[
@@ -329,7 +335,7 @@
         ]
         + [pl.BlockSpec(memory_space=pl.ANY)] * len(after),
         out_specs=(
-            pl.BlockSpec((n_span, MESH_X * PAIRS, 2 * zl), lambda g: (0, g, 0)),
+            pl.BlockSpec((n_span, MESH_X * pairs, 2 * zl), lambda g: (0, g, 0)),
             pl.BlockSpec(DONE.shape, lambda g: (0, 0)),
         ),
         compiler_params=pltpu.CompilerParams(vmem_limit_bytes=VMEM_BYTES),
@@ -338,7 +344,7 @@
     )(binary, dref, species, laplacian, perm, *after)
 
 
-def unpack_kernel(part, recv_ref, perm_ref, *refs):
+def unpack_kernel(part, n_nodes, recv_ref, perm_ref, *refs):
     out_ref = refs[-1]
     n_span = recv_ref.shape[0]
     per_step, _, zl, _ = out_ref.shape
@@ -351,9 +357,9 @@
             both, perm, (((0,), (0,)), ((), ())), preferred_element_type=f32
         )
 
-    def blocks():
+    def blocks(count=None):
         pairs = per_step // 2
-        for k in range(pairs):
+        for k in range(pairs if count is None else count):
             tile = jnp.concatenate(
                 [recv_ref[q, block_rows(part, k, pairs), :] for q in range(n_span)], axis=0
             )
@@ -363,11 +369,14 @@
 
     def tail():
         half = MESH_X // 2
+        left = before_tail(n_nodes, per_step)
+        blocks(left // 2)
+        row = left // 2 * MESH_X
         sides = []
         for q in range(n_span):
-            block = recv_ref[q, :half, :]
+            block = recv_ref[q, row : row + half, :]
             sides += [block, pltpu.roll(block, zl, 1)]
-        out_ref[0, 0] = turned(jnp.concatenate(sides, axis=0))[:zl]
+        out_ref[left, 0] = turned(jnp.concatenate(sides, axis=0))[:zl]
 
     by_step(part > 0, blocks, tail)
 
@@ -375,15 +384,15 @@
 def unpacked(s, part, recv, perm2, shape, before):
     n_nodes, n_species, zl, own = shape
     n_span, _, width = recv.shape
-    step = 2 * PAIRS
-    begin, steps, _ = part_blocks(n_nodes, part)
+    begin, steps, _, pairs = part_blocks(n_nodes, part)
+    step = 2 * pairs
     operands = [recv, perm2] + ([] if before is None else [before])
     return pl.pallas_call(
-        functools.partial(unpack_kernel, part),
+        functools.partial(unpack_kernel, part, n_nodes),
         grid=(steps,),
         out_shape=jax.ShapeDtypeStruct(shape, f32),
         in_specs=[
-            pl.BlockSpec((n_span, MESH_X * PAIRS, width), lambda g: (0, g, 0)),
+            pl.BlockSpec((n_span, MESH_X * pairs, width), lambda g: (0, g, 0)),
             pl.BlockSpec((2 * own, own), lambda g: (0, 0)),
         ]
         + ([] if before is None else [pl.BlockSpec(memory_space=pl.ANY)]),
@@ -711,7 +720,7 @@
     diag = 1.0 / (shifts[:, None, :] + eig_sum[None, :, None])
     rounds_row = jnp.tile(rounds, 2).reshape(1, planes)
 
-    in_parts = [(WHOLE,) if FIRST_WHOLE and s == 0 else (0, 1) for s in range(n_species)]
+    in_parts = [(WHOLE,) if s == 0 else (0, 1) for s in range(n_species)]
     out_parts = [(WHOLE,) if s + 1 == n_species else (0, 1) for s in range(n_species)]
     steps, count = [], 0
     arrived_by, slots, back_slots = [], [], []
@@ -734,7 +743,7 @@
     for arrival, _, _, s, (kind, index) in sorted(steps):
         if arrival > last and waiting:
             final = len(moved) + 1 == count
-            moved.append(across(released(waiting.pop(0), mark + (moved[-1:] if final else []))))
+            moved.append(across(released(waiting.pop(0), mark + ([moved[-1][0, :8]] if final else []))))
         last = arrival
         after = mark + (moved[arrival : arrival + 1] if arrival >= 0 else [])
         if kind == "pack":

time: 444 us -> 442 us (level)
  no operation moved by 1% of the time
where the time goes in v1:
time: 442 us; the launch traced here: 433 us
  waiting for transfers between devices  186 us (42%)
  Pallas kernels  162 us (37%)
  starting transfers between devices  65.4 us (15%)
  local copies, waits for them, and re-layouts  15.5 us (4%)
    all_to_all x10, waiting for transfers between devices, across(): return lax.all_to_all(sent, 'span', split_axis=0, concat_axis=0, tiled=True)  186 us
    pallas_call x12, Pallas kernels, vmem_call(): pl.pallas_call(ordered, out_shape=tuple(out_shape) + (DONE,), in_specs=[v...  118 us
    all_to_all x10, starting transfers between devices, across(): return lax.all_to_all(sent, 'span', split_axis=0, concat_axis=0, tiled=True)  45.1 us
    pallas_call x5, Pallas kernels, packed_source(): pl.pallas_call(functools.partial(source_kernel, s, part, n_nodes), grid=(...  24.2 us
    ppermute x9, starting transfers between devices, exchange(): below = lax.ppermute(up, axes, ring_route(n_span, n_elem, 1))  17.2 us
    pallas_call x5, Pallas kernels, unpacked(): pl.pallas_call(functools.partial(unpack_kernel, part, n_nodes), grid=(ste...  13.8 us
    unnamed x71, local copies, waits for them, and re-layouts  9.93 us
  transfers between devices with their start and end apart: 28, of which 11 were waited for; matrix products, arithmetic and copies ran while one was open for 2% of the time, Pallas kernels for 35%

profile of v1, /device:TPU:0, one launch (start us, length us, event | category | flops | bytes accessed | tf_op | source)
XLA Modules:
  0.0 432.8 jit_solution(13975974682360617547)
XLA Ops:
  0.0 2.5 mesh_tables.1
  2.5 6.4 %packed_source.5 = (f32[8,648,128]{2,1,0:T(8,128)}, f32[8,128]{1,0:T(8,128)}) custom-call(f32[3,4]{1,0:T(4,128)} %binary_ref.9, f32[3]{0:T(128)} %dref_ref.9, f32[81,3,64,128]{3,2,1,0:T(8,128)} %species_ref.9, f32[81,3,64,128]{3,2,1,0:T(8,128)} %lap_ref.9, bf16[128,256]{1,0:T(8,128)(2,1)} %get-tuple-element.80.perm_ref), custom_call_target="tpu_custom_call" | custom-call | flops 23000000512 | tf_op jit(solution)/shard_map/packed_source/pallas_call | solution.py:325
  8.9 7.3 %all-to-all-start = ((f32[8,648,128]{2,1,0:T(8,128)}), f32[8,648,128]{2,1,0:T(8,128)S(1)}, u32[]{:S(2)}, u32[]{:S(2)}) async-start(f32[8,648,128]{2,1,0:T(8,128)} %released.10), calls=%async_computation | async-start | bytes 5308416 | tf_op jit(solution)/shard_map/all_to_all | solution.py:710
  16.2 3.5 packed_source.6
  22.5 0.7 copy.49.refs_5_.refs_6_
  24.0 0.8 copy.38.refs_4_.refs_5_
  24.8 5.3 %packed_source.7 = (f32[8,392,128]{2,1,0:T(8,128)}, f32[8,128]{1,0:T(8,128)}) custom-call(f32[3,4]{1,0:T(4,128)} %binary_ref.9, f32[3]{0:T(128)} %dref_ref.9, f32[81,3,64,128]{3,2,1,0:T(8,128)} %species_ref.9, f32[81,3,64,128]{3,2,1,0:T(8,128)} %lap_ref.9, bf16[128,256]{1,0:T(8,128)(2,1)} %get-tuple-element.80.perm_ref, f32[8,128]{1,0:T(8,128)} %get-tuple-element.82.refs_0_), custom_call_target="tpu_custom_call" | custom-call | flops 23000000512 | tf_op jit(solution)/shard_map/packed_source/pallas_call | solution.py:325
  30.2 3.5 packed_source.8
  33.7 5.4 %packed_source.9 = (f32[8,392,128]{2,1,0:T(8,128)}, f32[8,128]{1,0:T(8,128)}) custom-call(f32[3,4]{1,0:T(4,128)} %binary_ref.9, f32[3]{0:T(128)} %dref_ref.9, f32[81,3,64,128]{3,2,1,0:T(8,128)} %species_ref.9, f32[81,3,64,128]{3,2,1,0:T(8,128)} %lap_ref.9, bf16[128,256]{1,0:T(8,128)(2,1)} %get-tuple-element.80.perm_ref, f32[8,128]{1,0:T(8,128)} %get-tuple-element.86.refs_0_), custom_call_target="tpu_custom_call" | custom-call | flops 23000000512 | tf_op jit(solution)/shard_map/packed_source/pallas_call | solution.py:325
  40.0 1.1 slice_bitcast_fusion
  41.1 3.6 link_matrices.1
  44.7 31.6 %all-to-all-done.refs_0_.refs_8_ = f32[8,648,128]{2,1,0:T(8,128)S(1)} async-done(((f32[8,648,128]{2,1,0:T(8,128)}), f32[8,648,128]{2,1,0:T(8,128)S(1)}, u32[]{:S(2)}, u32[]{:S(2)}) %all-to-all-start) | async-done | bytes 2654240 | tf_op jit(solution)/shard_map/all_to_all | solution.py:710
  76.3 4.2 all-to-all-start.1
  80.6 10.5 %start_solve.3 = (f32[1408,512]{1,0:T(8,128)}, f32[640,512]{1,0:T(8,128)}, f32[144,512]{1,0:T(8,128)}, f32[144,512]{1,0:T(8,128)}, f32[8,128]{1,0:T(8,128)}) custom-call(f32[8,648,128]{2,1,0:T(8,128)} %copy-done.7, bf16[512,512]{1,0:T(8,128)(2,1)} %constant.50.clone.refs_1_.refs_2_, bf16[512,512]{1,0:T(8,128)(2,1)} %constant.51.clone.refs_2_.refs_3_, ...), custom_call_target="tpu_custom_call" | custom-call | flops 92000002048 | tf_op jit(solution)/shard_map/start_solve/pallas_call | solution.py:586
  91.3 1.8 collective-permute-start.1
  94.5 11.7 %all-to-all-done.1.refs_11_.refs_0_ = f32[8,256,128]{2,1,0:T(8,128)} async-done(((f32[8,256,128]{2,1,0:T(8,128)}), f32[8,256,128]{2,1,0:T(8,128)}, u32[]{:S(2)}, u32[]{:S(2)}) %all-to-all-start.1) | async-done | bytes 1048608 | tf_op jit(solution)/shard_map/all_to_all | solution.py:710
  106.2 4.1 all-to-all-start.3
  110.3 0.7 copy-done.23
  111.1 8.1 %sweep_solve.6 = (f32[640,512]{1,0:T(8,128)}, f32[640,512]{1,0:T(8,128)}, f32[144,512]{1,0:T(8,128)}, f32[144,512]{1,0:T(8,128)}, f32[8,128]{1,0:T(8,128)}) custom-call(s32[1,512]{1,0:T(1,128)} %bitcast.22, f32[176,512]{1,0:T(8,128)} %get-tuple-element.146.refs_3_.refs_1_, bf16[640,928]{1,0:T(8,128)(2,1)} %get-tuple-element.78.refs_2_, ...), custom_call_target="tpu_custom_call" | custom-call | flops 57500000256 | tf_op jit(solution)/shard_map/sweep_solve/pallas_call | solution.py:586
  119.2 0.7 collective-permute-start.2
  119.9 1.6 collective-permute-start.3
  121.6 0.7 pad_maximum_fusion.refs_4_
  122.3 25.7 %all-to-all-done.3.refs_12_.refs_1_.refs_9_ = f32[8,392,128]{2,1,0:T(8,128)S(1)} async-done(((f32[8,392,128]{2,1,0:T(8,128)}), f32[8,392,128]{2,1,0:T(8,128)S(1)}, u32[]{:S(2)}, u32[]{:S(2)}) %all-to-all-start.3) | async-done | bytes 1605664 | tf_op jit(solution)/shard_map/all_to_all | solution.py:710
  147.9 4.7 %all-to-all-start.2 = ((f32[8,256,128]{2,1,0:T(8,128)}), f32[8,256,128]{2,1,0:T(8,128)}, u32[]{:S(2)}, u32[]{:S(2)}) async-start(f32[8,256,128]{2,1,0:T(8,128)} %released.12), calls=%async_computation.2 | async-start | bytes 2097152 | tf_op jit(solution)/shard_map/all_to_all | solution.py:710
  153.4 8.5 %sweep_solve.7 = (f32[640,512]{1,0:T(8,128)}, f32[640,512]{1,0:T(8,128)}, f32[144,512]{1,0:T(8,128)}, f32[144,512]{1,0:T(8,128)}, f32[8,128]{1,0:T(8,128)}) custom-call(s32[1,512]{1,0:T(1,128)} %bitcast.23, f32[176,512]{1,0:T(8,128)} %get-tuple-element.146.refs_3_.refs_1_, bf16[640,928]{1,0:T(8,128)(2,1)} %get-tuple-element.78.refs_2_, ...), custom_call_target="tpu_custom_call" | custom-call | flops 57500000256 | tf_op jit(solution)/shard_map/sweep_solve/pallas_call | solution.py:586
  162.0 0.8 collective-permute-start.6
  162.7 1.3 collective-permute-start.7
  164.1 10.0 %start_solve.4 = (f32[1408,512]{1,0:T(8,128)}, f32[640,512]{1,0:T(8,128)}, f32[144,512]{1,0:T(8,128)}, f32[144,512]{1,0:T(8,128)}, f32[8,128]{1,0:T(8,128)}) custom-call(f32[8,256,128]{2,1,0:T(8,128)} %all-to-all-done.1.refs_11_.refs_0_, f32[8,392,128]{2,1,0:T(8,128)} %copy-done.8, bf16[512,512]{1,0:T(8,128)(2,1)} %constant.50.clone.refs_1_.refs_2_, ...), custom_call_target="tpu_custom_call" | custom-call | flops 92000002048 | tf_op jit(solution)/shard_map/start_solve/pallas_call | solution.py:586
  174.4 1.6 collective-permute-start.5
  176.0 2.5 all-to-all-done.2.refs_13_.refs_11_.refs_0_
  178.6 4.5 %all-to-all-start.4 = ((f32[8,392,128]{2,1,0:T(8,128)}), f32[8,392,128]{2,1,0:T(8,128)}, u32[]{:S(2)}, u32[]{:S(2)}) async-start(f32[8,392,128]{2,1,0:T(8,128)} %released.14), calls=%async_computation.4 | async-start | bytes 3211264 | tf_op jit(solution)/shard_map/all_to_all | solution.py:710
  183.1 0.7 copy-done.17
  183.9 12.5 %finish_solve.3 = (f32[8,256,128]{2,1,0:T(8,128)}, f32[8,392,128]{2,1,0:T(8,128)}, f32[8,128]{1,0:T(8,128)}) custom-call(s32[1,512]{1,0:T(1,128)} %bitcast.24, f32[176,512]{1,0:T(8,128)} %get-tuple-element.146.refs_3_.refs_1_, bf16[640,928]{1,0:T(8,128)(2,1)} %get-tuple-element.78.refs_2_, bf16[352,80]{1,0:T(8,128)(2,1)} %pad_maximum_fusion.2.refs_4_.refs_3_, ...), custom_call_target="tpu_custom_call" | custom-call | flops 97749999616 | tf_op jit(solution)/shard_map/finish_solve/pallas_call | solution.py:586
  197.2 8.1 %sweep_solve.8 = (f32[640,512]{1,0:T(8,128)}, f32[640,512]{1,0:T(8,128)}, f32[144,512]{1,0:T(8,128)}, f32[144,512]{1,0:T(8,128)}, f32[8,128]{1,0:T(8,128)}) custom-call(s32[1,512]{1,0:T(1,128)} %bitcast.25, f32[176,512]{1,0:T(8,128)} %get-tuple-element.145.refs_4_.refs_1_, bf16[640,928]{1,0:T(8,128)(2,1)} %get-tuple-element.78.refs_2_, ...), custom_call_target="tpu_custom_call" | custom-call | flops 57500000256 | tf_op jit(solution)/shard_map/sweep_solve/pallas_call | solution.py:586
  205.9 2.0 collective-permute-start.9
  207.8 12.9 %all-to-all-done.4.refs_12_.refs_1_.refs_9_ = f32[8,392,128]{2,1,0:T(8,128)} async-done(((f32[8,392,128]{2,1,0:T(8,128)}), f32[8,392,128]{2,1,0:T(8,128)}, u32[]{:S(2)}, u32[]{:S(2)}) %all-to-all-start.4) | async-done | bytes 1605664 | tf_op jit(solution)/shard_map/all_to_all | solution.py:710
  220.7 4.3 all-to-all-start.5
  225.0 0.7 copy-done.30
  225.8 8.5 %sweep_solve.9 = (f32[640,512]{1,0:T(8,128)}, f32[640,512]{1,0:T(8,128)}, f32[144,512]{1,0:T(8,128)}, f32[144,512]{1,0:T(8,128)}, f32[8,128]{1,0:T(8,128)}) custom-call(s32[1,512]{1,0:T(1,128)} %bitcast.26, f32[176,512]{1,0:T(8,128)} %get-tuple-element.145.refs_4_.refs_1_, bf16[640,928]{1,0:T(8,128)(2,1)} %get-tuple-element.78.refs_2_, ...), custom_call_target="tpu_custom_call" | custom-call | flops 57500000256 | tf_op jit(solution)/shard_map/sweep_solve/pallas_call | solution.py:586
  234.7 2.3 collective-permute-start.13
  237.0 9.9 %start_solve.5 = (f32[1408,512]{1,0:T(8,128)}, f32[640,512]{1,0:T(8,128)}, f32[144,512]{1,0:T(8,128)}, f32[144,512]{1,0:T(8,128)}, f32[8,128]{1,0:T(8,128)}) custom-call(f32[8,256,128]{2,1,0:T(8,128)} %all-to-all-done.2.refs_13_.refs_11_.refs_0_, f32[8,392,128]{2,1,0:T(8,128)} %all-to-all-done.4.refs_12_.refs_1_.refs_9_, ...), custom_call_target="tpu_custom_call" | custom-call | flops 92000002048 | tf_op jit(solution)/shard_map/start_solve/pallas_call | solution.py:586
  247.0 2.0 collective-permute-start.11
  249.0 1.7 all-to-all-done.5.refs_13_.refs_11_.recv_ref
  250.7 4.3 all-to-all-start.6
  255.8 12.6 %finish_solve.4 = (f32[8,256,128]{2,1,0:T(8,128)}, f32[8,392,128]{2,1,0:T(8,128)}, f32[8,128]{1,0:T(8,128)}) custom-call(s32[1,512]{1,0:T(1,128)} %bitcast.27, f32[176,512]{1,0:T(8,128)} %get-tuple-element.145.refs_4_.refs_1_, bf16[640,928]{1,0:T(8,128)(2,1)} %get-tuple-element.78.refs_2_, bf16[352,80]{1,0:T(8,128)(2,1)} %pad_maximum_fusion.2.refs_4_.refs_3_, ...), custom_call_target="tpu_custom_call" | custom-call | flops 97749999616 | tf_op jit(solution)/shard_map/finish_solve/pallas_call | solution.py:586
  269.3 8.1 %sweep_solve.10 = (f32[640,512]{1,0:T(8,128)}, f32[640,512]{1,0:T(8,128)}, f32[144,512]{1,0:T(8,128)}, f32[144,512]{1,0:T(8,128)}, f32[8,128]{1,0:T(8,128)}) custom-call(s32[1,512]{1,0:T(1,128)} %bitcast.28, f32[176,512]{1,0:T(8,128)} %get-tuple-element.147.refs_4_.refs_1_, bf16[640,928]{1,0:T(8,128)(2,1)} %get-tuple-element.78.refs_2_, ...), custom_call_target="tpu_custom_call" | custom-call | flops 57500000256 | tf_op jit(solution)/shard_map/sweep_solve/pallas_call | solution.py:586
  277.4 2.5 collective-permute-start.15
  279.8 12.3 %all-to-all-done.6.refs_12_.recv_ref = f32[8,392,128]{2,1,0:T(8,128)} async-done(((f32[8,392,128]{2,1,0:T(8,128)}), f32[8,392,128]{2,1,0:T(8,128)}, u32[]{:S(2)}, u32[]{:S(2)}) %all-to-all-start.6) | async-done | bytes 1605664 | tf_op jit(solution)/shard_map/all_to_all | solution.py:710
  292.2 4.5 %all-to-all-start.7 = ((f32[8,256,128]{2,1,0:T(8,128)}), f32[8,256,128]{2,1,0:T(8,128)S(1)}, u32[]{:S(2)}, u32[]{:S(2)}) async-start(f32[8,256,128]{2,1,0:T(8,128)} %released.17), calls=%async_computation.7 | async-start | bytes 2097152 | tf_op jit(solution)/shard_map/all_to_all | solution.py:710
  296.7 0.7 copy-done.29
  297.5 8.5 %sweep_solve.11 = (f32[640,512]{1,0:T(8,128)}, f32[640,512]{1,0:T(8,128)}, f32[144,512]{1,0:T(8,128)}, f32[144,512]{1,0:T(8,128)}, f32[8,128]{1,0:T(8,128)}) custom-call(s32[1,512]{1,0:T(1,128)} %bitcast.29, f32[176,512]{1,0:T(8,128)} %get-tuple-element.147.refs_4_.refs_1_, bf16[640,928]{1,0:T(8,128)(2,1)} %get-tuple-element.78.refs_2_, ...), custom_call_target="tpu_custom_call" | custom-call | flops 57500000256 | tf_op jit(solution)/shard_map/sweep_solve/pallas_call | solution.py:586
  306.1 2.2 collective-permute-start.17
  308.3 13.7 %all-to-all-done.7.refs_13_.recv_ref = f32[8,256,128]{2,1,0:T(8,128)S(1)} async-done(((f32[8,256,128]{2,1,0:T(8,128)}), f32[8,256,128]{2,1,0:T(8,128)S(1)}, u32[]{:S(2)}, u32[]{:S(2)}) %all-to-all-start.7) | async-done | bytes 1048608 | tf_op jit(solution)/shard_map/all_to_all | solution.py:710
  322.0 1.0 copy-done.4
  323.0 3.6 all-to-all-start.8
  327.4 12.9 %finish_solve.5 = (f32[8,648,128]{2,1,0:T(8,128)}, f32[8,128]{1,0:T(8,128)}) custom-call(s32[1,512]{1,0:T(1,128)} %bitcast.30, f32[176,512]{1,0:T(8,128)} %get-tuple-element.147.refs_4_.refs_1_, bf16[640,928]{1,0:T(8,128)(2,1)} %get-tuple-element.78.refs_2_, bf16[352,80]{1,0:T(8,128)(2,1)} %pad_maximum_fusion.2.refs_4_.refs_3_, ...), custom_call_target="tpu_custom_call" | custom-call | flops 97749999616 | tf_op jit(solution)/shard_map/finish_solve/pallas_call | solution.py:586
  340.3 23.9 %all-to-all-done.8.recv_ref = f32[8,392,128]{2,1,0:T(8,128)S(1)} async-done(((f32[8,392,128]{2,1,0:T(8,128)}), f32[8,392,128]{2,1,0:T(8,128)S(1)}, u32[]{:S(2)}, u32[]{:S(2)}) %all-to-all-start.8) | async-done | bytes 1605664 | tf_op jit(solution)/shard_map/all_to_all | solution.py:710
  365.4 3.8 all-to-all-start.9
  369.2 2.6 unpacked.5.refs_0_
  371.8 4.1 unpacked.6.refs_0_
  375.9 1.6 unpacked.7.refs_0_
  377.5 2.6 unpacked.8.refs_0_
  380.1 49.4 %all-to-all-done.9.recv_ref = f32[8,648,128]{2,1,0:T(8,128)S(1)} async-done(((f32[8,648,128]{2,1,0:T(8,128)}), f32[8,648,128]{2,1,0:T(8,128)S(1)}, u32[]{:S(2)}, u32[]{:S(2)}) %all-to-all-start.9) | async-done | bytes 2654240 | tf_op jit(solution)/shard_map/all_to_all | solution.py:710
  429.5 2.9 unpacked.9
  (127 shorter events, 13.1 us)
Async XLA Ops:
  0.0 93.1 %copy-start = (s32[256]{0:T(256)S(1)}, s32[256]{0:T(256)}, u32[]{:S(2)}) copy-start(s32[256]{0:T(256)} %param.28) | copy-start | bytes 3076
  8.9 67.4 %all-to-all-start = ((f32[8,648,128]{2,1,0:T(8,128)}), f32[8,648,128]{2,1,0:T(8,128)S(1)}, u32[]{:S(2)}, u32[]{:S(2)}) async-start(f32[8,648,128]{2,1,0:T(8,128)} %released.10), calls=%async_computation | async-start | bytes 5308416 | tf_op jit(solution)/shard_map/all_to_all | solution.py:710
  16.2 3.6 copy-start.13
  16.2 3.6 copy-start.14
  16.2 3.6 copy-start.12
  16.2 3.8 copy-start.11
  39.1 0.7 copy-start.33
  76.3 4.2 copy-start.7
  76.3 29.9 %all-to-all-start.1 = ((f32[8,256,128]{2,1,0:T(8,128)}), f32[8,256,128]{2,1,0:T(8,128)}, u32[]{:S(2)}, u32[]{:S(2)}) async-start(f32[8,256,128]{2,1,0:T(8,128)} %released.11), calls=%async_computation.1 | async-start | bytes 2097152 | tf_op jit(solution)/shard_map/all_to_all | solution.py:710
  80.6 13.1 %copy-start.10 = (f32[88,40]{1,0:T(8,128)S(1)}, f32[88,40]{1,0:T(8,128)}, u32[]{:S(2)}) copy-start(f32[88,40]{1,0:T(8,128)} %get-tuple-element.155) | copy-start | bytes 42244
  91.1 19.2 %collective-permute-start = (f32[144,512]{1,0:T(8,128)}, f32[144,512]{1,0:T(8,128)S(1)}, u32[]{:S(2)}, u32[]{:S(2)}) collective-permute-start(f32[144,512]{1,0:T(8,128)} %get-tuple-element.89), channel_id=1, source_target_pairs={{0,3},{4,0},{12,4},{8,12},{16,8},{20,16},{28,20},{24,28},{25,24},{... | collective-permute-start | bytes 884744 | tf_op jit(solution)/shard_map/ppermute | solution.py:640
  91.3 19.0 %collective-permute-start.1 = (f32[144,512]{1,0:T(8,128)}, f32[144,512]{1,0:T(8,128)S(1)}, u32[]{:S(2)}, u32[]{:S(2)}) collective-permute-start(f32[144,512]{1,0:T(8,128)} %get-tuple-element.90), channel_id=1, source_target_pairs={{0,4},{4,12},{12,8},{8,16},{16,20},{20,28},{28,24},{24,25},{25,29}... | collective-permute-start | bytes 884744 | tf_op jit(solution)/shard_map/ppermute | solution.py:639
  106.2 41.7 %all-to-all-start.3 = ((f32[8,392,128]{2,1,0:T(8,128)}), f32[8,392,128]{2,1,0:T(8,128)S(1)}, u32[]{:S(2)}, u32[]{:S(2)}) async-start(f32[8,392,128]{2,1,0:T(8,128)} %released.13), calls=%async_computation.3 | async-start | bytes 3211264 | tf_op jit(solution)/shard_map/all_to_all | solution.py:710
  110.3 0.7 copy-start.23
  110.3 0.8 copy-start.25
  111.1 10.3 %copy-start.9 = (f32[88,88]{1,0:T(8,128)S(1)}, f32[88,88]{1,0:T(8,128)}, u32[]{:S(2)}) copy-start(f32[88,88]{1,0:T(8,128)} %get-tuple-element.151) | copy-start | bytes 92932
  119.2 33.4 %collective-permute-start.2 = (f32[144,512]{1,0:T(8,128)}, f32[144,512]{1,0:T(8,128)S(1)}, u32[]{:S(2)}, u32[]{:S(2)}) collective-permute-start(f32[144,512]{1,0:T(8,128)} %get-tuple-element.97), channel_id=1, source_target_pairs={{0,3},{4,0},{12,4},{8,12},{16,8},{20,16},{28,20},{24,28},{25,24},{... | collective-permute-start | bytes 884744 | tf_op jit(solution)/shard_map/ppermute | solution.py:640
  119.9 32.7 %collective-permute-start.3 = (f32[144,512]{1,0:T(8,128)}, f32[144,512]{1,0:T(8,128)S(1)}, u32[]{:S(2)}, u32[]{:S(2)}) collective-permute-start(f32[144,512]{1,0:T(8,128)} %get-tuple-element.98), channel_id=1, source_target_pairs={{0,4},{4,12},{12,8},{8,16},{16,20},{20,28},{28,24},{24,25},{25,29}... | collective-permute-start | bytes 884744 | tf_op jit(solution)/shard_map/ppermute | solution.py:639
  147.9 4.7 %copy-start.8 = (f32[8,392,128]{2,1,0:T(8,128)}, f32[8,392,128]{2,1,0:T(8,128)S(1)}, u32[]{:S(2)}) copy-start(f32[8,392,128]{2,1,0:T(8,128)S(1)} %all-to-all-done.3.refs_12_.refs_1_.refs_9_) | copy-start | bytes 4816900
  147.9 30.6 %all-to-all-start.2 = ((f32[8,256,128]{2,1,0:T(8,128)}), f32[8,256,128]{2,1,0:T(8,128)}, u32[]{:S(2)}, u32[]{:S(2)}) async-start(f32[8,256,128]{2,1,0:T(8,128)} %released.12), calls=%async_computation.2 | async-start | bytes 2097152 | tf_op jit(solution)/shard_map/all_to_all | solution.py:710
  152.6 0.7 copy-start.24
  152.6 0.8 copy-start.26
  162.0 21.1 %collective-permute-start.6 = (f32[144,512]{1,0:T(8,128)}, f32[144,512]{1,0:T(8,128)S(1)}, u32[]{:S(2)}, u32[]{:S(2)}) collective-permute-start(f32[144,512]{1,0:T(8,128)} %get-tuple-element.106), channel_id=1, source_target_pairs={{0,3},{4,0},{12,4},{8,12},{16,8},{20,16},{28,20},{24,28},{25,24},{... | collective-permute-start | bytes 884744 | tf_op jit(solution)/shard_map/ppermute | solution.py:640
  162.7 20.3 %collective-permute-start.7 = (f32[144,512]{1,0:T(8,128)}, f32[144,512]{1,0:T(8,128)S(1)}, u32[]{:S(2)}, u32[]{:S(2)}) collective-permute-start(f32[144,512]{1,0:T(8,128)} %get-tuple-element.107), channel_id=1, source_target_pairs={{0,4},{4,12},{12,8},{8,16},{16,20},{20,28},{28,24},{24,25},{25,29}... | collective-permute-start | bytes 884744 | tf_op jit(solution)/shard_map/ppermute | solution.py:639
  174.0 22.4 %collective-permute-start.4 = (f32[144,512]{1,0:T(8,128)}, f32[144,512]{1,0:T(8,128)S(1)}, u32[]{:S(2)}, u32[]{:S(2)}) collective-permute-start(f32[144,512]{1,0:T(8,128)} %get-tuple-element.103), channel_id=1, source_target_pairs={{0,3},{4,0},{12,4},{8,12},{16,8},{20,16},{28,20},{24,28},{25,24},{... | collective-permute-start | bytes 884744 | tf_op jit(solution)/shard_map/ppermute | solution.py:640
  174.4 22.0 %collective-permute-start.5 = (f32[144,512]{1,0:T(8,128)}, f32[144,512]{1,0:T(8,128)S(1)}, u32[]{:S(2)}, u32[]{:S(2)}) collective-permute-start(f32[144,512]{1,0:T(8,128)} %get-tuple-element.104), channel_id=1, source_target_pairs={{0,4},{4,12},{12,8},{8,16},{16,20},{20,28},{28,24},{24,25},{25,29}... | collective-permute-start | bytes 884744 | tf_op jit(solution)/shard_map/ppermute | solution.py:639
  178.6 42.1 %all-to-all-start.4 = ((f32[8,392,128]{2,1,0:T(8,128)}), f32[8,392,128]{2,1,0:T(8,128)}, u32[]{:S(2)}, u32[]{:S(2)}) async-start(f32[8,392,128]{2,1,0:T(8,128)} %released.14), calls=%async_computation.4 | async-start | bytes 3211264 | tf_op jit(solution)/shard_map/all_to_all | solution.py:710
  183.1 0.7 copy-start.17
  183.1 0.8 copy-start.20
  196.4 0.7 copy-start.18
  196.4 0.8 copy-start.21
  205.4 19.6 %collective-permute-start.8 = (f32[144,512]{1,0:T(8,128)}, f32[144,512]{1,0:T(8,128)S(1)}, u32[]{:S(2)}, u32[]{:S(2)}) collective-permute-start(f32[144,512]{1,0:T(8,128)} %get-tuple-element.112), channel_id=1, source_target_pairs={{0,3},{4,0},{12,4},{8,12},{16,8},{20,16},{28,20},{24,28},{25,24},{... | collective-permute-start | bytes 884744 | tf_op jit(solution)/shard_map/ppermute | solution.py:640
  205.9 19.1 %collective-permute-start.9 = (f32[144,512]{1,0:T(8,128)}, f32[144,512]{1,0:T(8,128)S(1)}, u32[]{:S(2)}, u32[]{:S(2)}) collective-permute-start(f32[144,512]{1,0:T(8,128)} %get-tuple-element.113), channel_id=1, source_target_pairs={{0,4},{4,12},{12,8},{8,16},{16,20},{20,28},{28,24},{24,25},{25,29}... | collective-permute-start | bytes 884744 | tf_op jit(solution)/shard_map/ppermute | solution.py:639
  220.7 30.0 %all-to-all-start.5 = ((f32[8,256,128]{2,1,0:T(8,128)}), f32[8,256,128]{2,1,0:T(8,128)}, u32[]{:S(2)}, u32[]{:S(2)}) async-start(f32[8,256,128]{2,1,0:T(8,128)} %released.15), calls=%async_computation.5 | async-start | bytes 2097152 | tf_op jit(solution)/shard_map/all_to_all | solution.py:710
  225.0 0.7 copy-start.30
  225.0 0.8 copy-start.32
  234.4 20.6 %collective-permute-start.12 = (f32[144,512]{1,0:T(8,128)}, f32[144,512]{1,0:T(8,128)S(1)}, u32[]{:S(2)}, u32[]{:S(2)}) collective-permute-start(f32[144,512]{1,0:T(8,128)} %get-tuple-element.121), channel_id=1, source_target_pairs={{0,3},{4,0},{12,4},{8,12},{16,8},{20,16},{28,20},{24,28},{25,24},{... | collective-permute-start | bytes 884744 | tf_op jit(solution)/shard_map/ppermute | solution.py:640
  234.7 20.3 %collective-permute-start.13 = (f32[144,512]{1,0:T(8,128)}, f32[144,512]{1,0:T(8,128)S(1)}, u32[]{:S(2)}, u32[]{:S(2)}) collective-permute-start(f32[144,512]{1,0:T(8,128)} %get-tuple-element.122), channel_id=1, source_target_pairs={{0,4},{4,12},{12,8},{8,16},{16,20},{20,28},{28,24},{24,25},{25,29}... | collective-permute-start | bytes 884744 | tf_op jit(solution)/shard_map/ppermute | solution.py:639
  247.0 21.5 %collective-permute-start.10 = (f32[144,512]{1,0:T(8,128)}, f32[144,512]{1,0:T(8,128)S(1)}, u32[]{:S(2)}, u32[]{:S(2)}) collective-permute-start(f32[144,512]{1,0:T(8,128)} %get-tuple-element.118), channel_id=1, source_target_pairs={{0,3},{4,0},{12,4},{8,12},{16,8},{20,16},{28,20},{24,28},{25,24},{... | collective-permute-start | bytes 884744 | tf_op jit(solution)/shard_map/ppermute | solution.py:640
  247.0 21.5 %collective-permute-start.11 = (f32[144,512]{1,0:T(8,128)}, f32[144,512]{1,0:T(8,128)S(1)}, u32[]{:S(2)}, u32[]{:S(2)}) collective-permute-start(f32[144,512]{1,0:T(8,128)} %get-tuple-element.119), channel_id=1, source_target_pairs={{0,4},{4,12},{12,8},{8,16},{16,20},{20,28},{28,24},{24,25},{25,29}... | collective-permute-start | bytes 884744 | tf_op jit(solution)/shard_map/ppermute | solution.py:639
  250.7 41.5 %all-to-all-start.6 = ((f32[8,392,128]{2,1,0:T(8,128)}), f32[8,392,128]{2,1,0:T(8,128)}, u32[]{:S(2)}, u32[]{:S(2)}) async-start(f32[8,392,128]{2,1,0:T(8,128)} %released.16), calls=%async_computation.6 | async-start | bytes 3211264 | tf_op jit(solution)/shard_map/all_to_all | solution.py:710
  255.0 0.7 copy-start.15
  255.0 0.8 copy-start.16
  268.4 0.7 copy-start.19
  268.5 0.7 copy-start.22
  277.3 19.3 %collective-permute-start.14 = (f32[144,512]{1,0:T(8,128)}, f32[144,512]{1,0:T(8,128)S(1)}, u32[]{:S(2)}, u32[]{:S(2)}) collective-permute-start(f32[144,512]{1,0:T(8,128)} %get-tuple-element.129), channel_id=1, source_target_pairs={{0,3},{4,0},{12,4},{8,12},{16,8},{20,16},{28,20},{24,28},{25,24},{... | collective-permute-start | bytes 884744 | tf_op jit(solution)/shard_map/ppermute | solution.py:640
  277.4 19.3 %collective-permute-start.15 = (f32[144,512]{1,0:T(8,128)}, f32[144,512]{1,0:T(8,128)S(1)}, u32[]{:S(2)}, u32[]{:S(2)}) collective-permute-start(f32[144,512]{1,0:T(8,128)} %get-tuple-element.130), channel_id=1, source_target_pairs={{0,4},{4,12},{12,8},{8,16},{16,20},{20,28},{28,24},{24,25},{25,29}... | collective-permute-start | bytes 884744 | tf_op jit(solution)/shard_map/ppermute | solution.py:639
  292.2 29.8 %all-to-all-start.7 = ((f32[8,256,128]{2,1,0:T(8,128)}), f32[8,256,128]{2,1,0:T(8,128)S(1)}, u32[]{:S(2)}, u32[]{:S(2)}) async-start(f32[8,256,128]{2,1,0:T(8,128)} %released.17), calls=%async_computation.7 | async-start | bytes 2097152 | tf_op jit(solution)/shard_map/all_to_all | solution.py:710
  296.7 0.7 copy-start.29
  296.7 0.8 copy-start.31
  306.0 20.5 %collective-permute-start.16 = (f32[144,512]{1,0:T(8,128)}, f32[144,512]{1,0:T(8,128)S(1)}, u32[]{:S(2)}, u32[]{:S(2)}) collective-permute-start(f32[144,512]{1,0:T(8,128)} %get-tuple-element.135), channel_id=1, source_target_pairs={{0,3},{4,0},{12,4},{8,12},{16,8},{20,16},{28,20},{24,28},{25,24},{... | collective-permute-start | bytes 884744 | tf_op jit(solution)/shard_map/ppermute | solution.py:640
  306.1 20.5 %collective-permute-start.17 = (f32[144,512]{1,0:T(8,128)}, f32[144,512]{1,0:T(8,128)S(1)}, u32[]{:S(2)}, u32[]{:S(2)}) collective-permute-start(f32[144,512]{1,0:T(8,128)} %get-tuple-element.136), channel_id=1, source_target_pairs={{0,4},{4,12},{12,8},{8,16},{16,20},{20,28},{28,24},{24,25},{25,29}... | collective-permute-start | bytes 884744 | tf_op jit(solution)/shard_map/ppermute | solution.py:639
  322.0 1.0 copy-start.4
  323.0 41.3 %all-to-all-start.8 = ((f32[8,392,128]{2,1,0:T(8,128)}), f32[8,392,128]{2,1,0:T(8,128)S(1)}, u32[]{:S(2)}, u32[]{:S(2)}) async-start(f32[8,392,128]{2,1,0:T(8,128)} %released.18), calls=%async_computation.8 | async-start | bytes 3211264 | tf_op jit(solution)/shard_map/all_to_all | solution.py:710
  326.6 0.7 copy-start.27
  326.6 0.8 copy-start.28
  364.2 1.2 copy-start.2
  365.4 3.8 copy-start.6
  365.4 64.1 %all-to-all-start.9 = ((f32[8,648,128]{2,1,0:T(8,128)}), f32[8,648,128]{2,1,0:T(8,128)S(1)}, u32[]{:S(2)}, u32[]{:S(2)}) async-start(f32[8,648,128]{2,1,0:T(8,128)} %released.19), calls=%async_computation.9 | async-start | bytes 5308416 | tf_op jit(solution)/shard_map/all_to_all | solution.py:710
  371.8 4.1 copy-start.5
  375.9 1.6 copy-start.3
  429.5 2.9 copy-start.1
